TPU v7x, 512 devices: a whole 4x4x16 slice. The times are simulated.
512 devices in a mesh: rep: 64 (over y_hi, z, core), shard: 8 (over x, y_lo).
Axes of the slice: x: 4, y: 4 (y_hi: 2, y_lo: 2; y = y_hi * 2 + y_lo), z: 16, core: 2. Of those that a mesh axis runs over, the one named last changes fastest.
Arguments:
- gradients: bfloat16 [64, 32, 128, 128], P('rep', 'shard'), may hold values from -6 to 6
- momentum: float32 [64, 32, 128, 128], P('rep', 'shard'), may hold values from -12 to 12
- params: bfloat16 [32, 128, 128], P('shard'), may hold values from -3 to 3
- band_offsets: int32 [32, 2], P('shard'), may hold values from 0 to 112
Outputs:
- new_momentum: float32 [64, 32, 128, 128], P('rep', 'shard')
- new_params: bfloat16 [32, 128, 128], replicated
All inputs are finite; a program needn't handle non-finite values.
Results may differ from a plain program's by a relative error of at most 0.001.
Values may be sent and summed in bfloat16 or wider, within the bound.
No kernel may reach another device: no remote copies, remote signals or barrier semaphores. Data moves between devices by JAX's collectives and lax.ppermute only.
A program may use at most 64 MiB of HBM per device.

v0:
```python
import math

import jax
import jax.numpy as jnp
from jax import lax
from jax.sharding import PartitionSpec as P

BAND = 16


def dct_entries(freq, length):
    kval = freq.astype(jnp.float32)[..., None]
    place = jnp.arange(length, dtype=jnp.float32)
    factor = jnp.where(kval == 0, math.sqrt(1.0 / length), math.sqrt(2.0 / length))
    return factor * jnp.cos(math.pi * (place + 0.5) * kval / length)


def band_tables(offsets, length, width):
    steps = jnp.arange(width, dtype=jnp.int32)
    rows_tab = dct_entries(offsets[:, 0:1] + steps[None, :], length)
    cols_tab = dct_entries(offsets[:, 1:2] + steps[None, :], length)
    return (rows_tab, cols_tab)


def apply_update(tiles, rows_tab, cols_tab, average):
    highest = lax.Precision.HIGHEST
    half = jnp.einsum("tik,tij->tkj", rows_tab, average, precision=highest)
    update = jnp.einsum("tkj,tjl->tkl", half, cols_tab, precision=highest)
    scale = jnp.sqrt(jnp.mean(update * update, axis=(1, 2), keepdims=True) + 1e-06)
    return (tiles.astype(jnp.float32) - update / scale).astype(jnp.bfloat16)


def per_device(gradients, momentum, params, band_offsets):
    highest = lax.Precision.HIGHEST
    length = params.shape[1]
    width = BAND
    rows_tab, cols_tab = band_tables(band_offsets, length, width)
    moment = 0.9 * momentum[0] + gradients[0].astype(jnp.float32)
    left = jnp.einsum("tik,tkl->til", rows_tab, moment, precision=highest)
    bands = jnp.einsum("til,tjl->tij", left, cols_tab, precision=highest)
    back = jnp.einsum("tik,tij->tkj", rows_tab, bands, precision=highest)
    local = jnp.einsum("tkj,tjl->tkl", back, cols_tab, precision=highest)
    new_momentum = (moment - local)[None]
    total = lax.psum(bands, "rep")
    average = total / lax.axis_size("rep")
    fresh = apply_update(params, rows_tab, cols_tab, average)
    whole = lax.all_gather(fresh, "shard", axis=0, tiled=True)
    return (new_momentum, whole)


def solution(mesh):
    in_specs = (
        P("rep", "shard", None, None),
        P("rep", "shard", None, None),
        P("shard", None, None),
        P("shard", None),
    )
    out_specs = (P("rep", "shard", None, None), P())
    return jax.shard_map(
        per_device, mesh=mesh, in_specs=in_specs, out_specs=out_specs, check_vma=False
    )
```

profile of v0, /device:TPU:1, one launch (start us, length us, event | category | flops | bytes accessed | tf_op | source)
XLA Modules:
  0.0 320.1 jit_solution(18132760493501453883)
XLA Ops:
  7.2 0.0 all-gather.2.cloned.1.call-start
  7.2 0.8 slice_bitcast_fusion
  8.0 0.1 compare_select_fusion
  8.0 0.1 add_convert_fusion
  8.1 1.5 fusion.1
  9.7 0.4 fusion.7
  10.0 262.6 %psum.7 = f32[4,16,16]{2,1,0:T(8,128)S(1)} all-reduce(f32[4,16,16]{2,1,0:T(8,128)S(1)} %fusion.7), channel_id=1, replica_groups=mesh['rep'=64,'shard'=8] {'rep'}, use_global_device_ids=true, to_apply=%region_0.1 | all-reduce | flops 1024 | bytes 8192 | tf_op jit(solution)/shard_map/psum | solution.py:44
  272.6 0.3 fusion.4
  273.0 0.0 copy-start.2
  273.0 0.8 multiply_reduce_fusion
  273.8 0.1 copy-done.2
  273.9 0.0 copy-start.1
  273.9 0.8 subtract_convert_fusion
  274.7 0.0 copy-start
  274.7 0.0 all-gather.2.cloned.1.call-update
  274.7 0.4 fusion.8
  275.1 0.0 copy-done.1
  275.1 0.6 copy-done
  275.6 1.4 fusion
  277.0 33.9 %all-gather.2.cloned.1.call-done = bf16[32,128,128]{2,1,0:T(8,128)(2,1)} async-done(((bf16[4,128,128]{2,1,0:T(8,128)(2,1)}), bf16[32,128,128]{2,1,0:T(8,128)(2,1)}) %all-gather.2.cloned.1.call-update) | async-done | bytes 1048592 | tf_op jit(solution)/shard_map/all_gather | solution.py:47
  310.9 2.3 copy.7
  (2 shorter events, 0.0 us)
Async XLA Ops:
  7.2 303.7 %all-gather.2.cloned.1.call-start = ((), (), s32[]{:S(2)}) async-start(), calls=%async_computation | async-start | bytes 1179648 | tf_op jit(solution)/shard_map/all_gather | solution.py:47
  273.0 0.9 copy-start.2
  273.9 1.2 copy-start.1
  274.7 1.0 copy-start
Sparse Core Ops, SparseCore 0:
  274.8 36.0 all-gather.1
where the time goes:
time: 325 us; the launch traced here: 320 us
  blocking collectives  263 us (81%)
  waiting for transfers between devices  33.9 us (10%)
  between operations  14.1 us (4%)
  matrix products  4.72 us (1%)
  local copies, waits for them, and re-layouts  3.77 us (1%)
    psum x1, blocking collectives, per_device(): total = lax.psum(bands, 'rep')  263 us
    all_gather x1, waiting for transfers between devices, per_device(): whole = lax.all_gather(fresh, 'shard', axis=0, tiled=True)  33.9 us
  transfers between devices with their start and end apart: 1, of which 1 were waited for; matrix products, arithmetic and copies ran while one was open for 1% of the time, Pallas kernels for 0%

commit v1 on v0

v1 whole, which is shorter than its diff:
```python
import functools
import math

import jax
import jax.numpy as jnp
import numpy as np
from jax import lax
from jax.experimental import pallas as pl
from jax.experimental.pallas import tpu as pltpu
from jax.sharding import Mesh, PartitionSpec as P

BAND = 16
TILE = 128
AXES = ("yh", "z", "core", "x", "yl")
PLANE = ("yh", "core", "x", "yl")
F32 = jnp.float32
BF16 = jnp.bfloat16
ROWS = 96


def cosine_table():
    k = np.arange(TILE, dtype=np.float64)[:, None]
    x = np.arange(TILE, dtype=np.float64)[None, :]
    factor = np.where(k == 0, math.sqrt(1.0 / TILE), math.sqrt(2.0 / TILE))
    return factor * np.cos(math.pi * (x + 0.5) * k / TILE)


def split_table():
    table = cosine_table().astype(np.float32)
    high = table.astype(jnp.bfloat16)
    low = (table - high.astype(np.float32)).astype(jnp.bfloat16)
    across = np.concatenate([high, low], axis=1)
    down = np.concatenate([high.T, low.T], axis=0)
    return across, down


def iota(shape, dim):
    return lax.broadcasted_iota(jnp.int32, shape, dim)


def dot(a, b):
    return lax.dot_general(a, b, (((1,), (0,)), ((), ())), preferred_element_type=F32)


def dot_nt(a, b):
    return lax.dot_general(a, b, (((1,), (1,)), ((), ())), preferred_element_type=F32)


def pieces(v):
    high = v.astype(BF16)
    low = (v - high.astype(F32)).astype(BF16)
    return high, low


def fold(v):
    return v[:, :TILE] + v[:, TILE:]


def wide(v):
    high, low = pieces(v)
    return jnp.concatenate([high, low], axis=1)


def weights(v):
    both = wide(v)
    return jnp.concatenate([both, both], axis=0)


def frequencies(offs_ref, which):
    lane = iota((1, TILE), 1)
    tile = (lane % 64) // BAND
    freq = lane % BAND
    for t in range(4):
        freq = freq + jnp.where(tile == t, offs_ref[t, which], 0)
    return freq


def tables(freq, down):
    picks = (iota((TILE, TILE), 0) == freq).astype(F32).astype(BF16)
    both = dot(down, picks)
    return both[:TILE].astype(BF16), both[TILE:].astype(BF16)


def moments(g_ref, m_ref):
    return 0.9 * m_ref[...] + g_ref[...].astype(F32)


def bands_kernel(offs_ref, g_ref, m_ref, across_ref, down_ref, packed_ref, bands_ref):
    lane = iota((1, TILE), 1)
    slot = (lane % 64) // BAND
    cols_high, cols_low = tables(frequencies(offs_ref, 1), down_ref[...])
    cols = jnp.concatenate([cols_high, cols_low], axis=1)
    cols = jnp.concatenate([cols, cols], axis=0)
    steps = iota((BAND, TILE), 1) - iota((BAND, TILE), 0)
    picks = jnp.concatenate([(steps == offs_ref[t, 0]).astype(F32) for t in range(4)], axis=0)
    rows = dot(picks.astype(BF16), across_ref[...]).astype(BF16)
    right = jnp.zeros((TILE, TILE), F32)
    for t in range(4):
        moment = 0.9 * m_ref[t] + g_ref[t].astype(F32)
        right = jnp.where(slot == t, fold(dot(wide(moment), cols)), right)
    every = fold(dot(rows, weights(right)))
    bands = jnp.zeros((BAND, TILE), F32)
    for t in range(4):
        bands = jnp.where(slot == t, every[BAND * t : BAND * t + BAND], bands)
    bands_ref[...] = bands
    packed_ref[...] = jnp.where(lane < 64, bands[:8], bands[8:])


def momentum_kernel(offs_ref, g_ref, m_ref, down_ref, bands_ref, out_ref):
    lane = iota((1, TILE), 1)
    rows = jnp.concatenate(tables(frequencies(offs_ref, 0), down_ref[...]), axis=1)
    cols_high, cols_low = tables(frequencies(offs_ref, 1), down_ref[...])
    cols = jnp.concatenate(
        [jnp.concatenate([cols_high, cols_high], axis=1), jnp.concatenate([cols_low, cols_low], axis=1)], axis=0
    )
    bands = bands_ref[...]
    diagonal = [jnp.where(lane // BAND == t, bands, 0.0) for t in range(4)]
    diagonal = jnp.concatenate(diagonal + [jnp.zeros((64, TILE), F32)], axis=0)
    half = wide(fold(dot(rows, weights(diagonal))))
    lanes = iota((1, 2 * TILE), 1)
    slot = (lanes % TILE) // BAND
    for t in range(4):
        moment = 0.9 * m_ref[t] + g_ref[t].astype(F32)
        own = jnp.where(slot == t, half.astype(F32), 0.0).astype(BF16)
        out_ref[t] = moment - fold(dot_nt(own, cols))


def block_kernel(offs_ref, got_ref, params_ref, out_ref):
    lane = iota((1, TILE), 1)
    first = lane < 64
    total = jnp.sum(got_ref[...], axis=0)
    turned = pltpu.roll(total, 64, 1)
    high, low = [p.astype(F32) for p in pieces(total)]
    turned_high, turned_low = [p.astype(F32) for p in pieces(turned)]
    bands = jnp.concatenate(
        [jnp.where(first, high, turned_low), jnp.where(first, turned_high, low)], axis=0
    ).astype(BF16)
    row = iota((BAND, TILE), 0)
    freq = jnp.where(row == 0, frequencies(offs_ref, 0), frequencies(offs_ref, 1))
    tail = jnp.concatenate([bands, freq.astype(F32).astype(BF16)], axis=0)
    quarter = 2 * lax.axis_index("yh") + lax.axis_index("core")
    for core in range(2):
        piece = params_ref[4 * core + quarter]
        for yh in range(2):
            for s in range(8):
                out_ref[(2 * yh + core) * 8 + s, :64] = piece
                out_ref[(2 * yh + core) * 8 + s, 64:] = tail


def update_kernel(own_ref, other_ref, down_ref, out_ref):
    lane = iota((1, TILE), 1)
    first = lane < 64
    down = down_ref[...]
    core = lax.axis_index("core")
    lanes = iota((1, 2 * TILE), 1)
    slot = (lanes % TILE) // BAND
    groups = []
    squares = []
    for g in range(4):
        sums = []
        for s in (2 * g, 2 * g + 1):
            v = own_ref[s, 64:80].astype(F32)
            for q in range(1, 4):
                v = v + own_ref[8 * q + s, 64:80].astype(F32)
            v = (v + pltpu.roll(v, 64, 1)) * (1.0 / 64)
            sums.append(v)
        groups.append(sums)
        both = jnp.where(first, sums[0], sums[1])
        squares.append(jnp.sum(both * both, axis=0, keepdims=True))
    squares = jnp.concatenate(squares + squares, axis=0)
    same = (iota((TILE, TILE), 0) // BAND == iota((TILE, TILE), 1) // BAND).astype(F32).astype(BF16)
    high, low = pieces(squares)
    mean = (dot(high, same) + dot(low, same)) * (1.0 / (TILE * TILE))
    inverse = 1.0 / jnp.sqrt(mean + 1e-06)
    for g in range(4):
        freqs = [own_ref[s, 80:96].astype(F32).astype(jnp.int32) for s in (2 * g, 2 * g + 1)]
        freqs = jnp.where(first, freqs[0], freqs[1])
        rows = jnp.concatenate(tables(freqs[0:1], down), axis=1)
        cols_high, cols_low = tables(freqs[1:2], down)
        cols = jnp.concatenate(
            [jnp.concatenate([cols_high, cols_high], axis=1), jnp.concatenate([cols_low, cols_low], axis=1)], axis=0
        )
        scaled = [v * inverse[g : g + 1] for v in groups[g]]
        diagonal = jnp.concatenate([jnp.where(lane // BAND == t, scaled[t // 4], 0.0) for t in range(8)], axis=0)
        half = wide(fold(dot(rows, weights(diagonal)))).astype(F32)
        for ref, half_of in ((own_ref, core), (other_ref, 1 - core)):
            for sh in range(2):
                for yh in range(2):
                    s = 2 * g + sh
                    tile = 2 * half_of + yh
                    own = jnp.where(slot == 4 * sh + tile, half, 0.0).astype(BF16)
                    update = fold(dot_nt(own, cols))
                    params = jnp.concatenate([ref[16 * yh + s, :64], ref[16 * yh + 8 + s, :64]], axis=0)
                    out_ref[4 * s + tile] = (params.astype(F32) - update).astype(BF16)


SMEM = pl.BlockSpec(memory_space=pltpu.SMEM)
VMEM = pl.BlockSpec(memory_space=pltpu.VMEM)
PARAMS = pltpu.CompilerParams(vmem_limit_bytes=40 * 1024 * 1024)


def per_device(gradients, momentum, params, band_offsets):
    across, down = [jnp.asarray(t) for t in split_table()]
    g, m = gradients[0], momentum[0]
    packed, bands = pl.pallas_call(
        bands_kernel,
        out_shape=(jax.ShapeDtypeStruct((8, TILE), F32), jax.ShapeDtypeStruct((BAND, TILE), F32)),
        in_specs=[SMEM, VMEM, VMEM, VMEM, VMEM],
        out_specs=(VMEM, VMEM),
        compiler_params=PARAMS,
        name="bands",
    )(band_offsets, g, m, across, down)
    got = lax.all_to_all(jnp.broadcast_to(packed[None], (16, 8, TILE)), "z", 0, 0)
    blocks = pl.pallas_call(
        block_kernel,
        out_shape=jax.ShapeDtypeStruct((32, ROWS, TILE), BF16),
        in_specs=[SMEM, VMEM, VMEM],
        out_specs=VMEM,
        compiler_params=PARAMS,
        name="blocks",
    )(band_offsets, got, params.reshape(8, 64, TILE))
    own = lax.all_to_all(blocks, PLANE, 0, 0)
    other = lax.ppermute(own, "core", [(0, 1), (1, 0)])
    new_momentum = pl.pallas_call(
        momentum_kernel,
        out_shape=jax.ShapeDtypeStruct((4, TILE, TILE), F32),
        in_specs=[SMEM, VMEM, VMEM, VMEM, VMEM],
        out_specs=VMEM,
        compiler_params=PARAMS,
        cost_estimate=pl.CostEstimate(flops=200_000_000, bytes_accessed=700_000, transcendentals=0),
        name="momentum",
    )(band_offsets, g, m, down, bands)
    whole = pl.pallas_call(
        update_kernel,
        out_shape=jax.ShapeDtypeStruct((32, TILE, TILE), BF16),
        in_specs=[VMEM, VMEM, VMEM],
        out_specs=VMEM,
        compiler_params=PARAMS,
        name="update",
    )(own, other, down)
    return (new_momentum[None], whole)


def solution(mesh):
    fine = Mesh(mesh.devices.reshape(2, 16, 2, 4, 2), AXES)
    rep, shard = ("yh", "z", "core"), ("x", "yl")
    in_specs = (P(rep, shard, None, None), P(rep, shard, None, None), P(shard, None, None), P(shard, None))
    out_specs = (P(rep, shard, None, None), P())
    return jax.shard_map(per_device, mesh=fine, in_specs=in_specs, out_specs=out_specs, check_vma=False)
```

time: 325 us -> 65.5 us (0.20); the launches traced: 320 us -> 65.2 us
  blocking collectives: 263 us -> 49.6 us
  waiting for transfers between devices: 33.9 us -> 0.06 us
  between operations: 14.1 us -> 0.73 us
  Pallas kernels: 0 us -> 7.02 us
  matrix products: 4.72 us -> 0 us
  starting transfers between devices: 0.04 us -> 3.39 us
    psum x1 -> x0, blocking collectives: 263 us -> none  [per_device(): total = lax.psum(bands, 'rep')]
    all_to_all x0 -> x2, blocking collectives: none -> 49.6 us  [the longest x1 27.2 us: per_device(): lax.all_to_all(jnp.broadcast_to(packed[None], (16, 8, TILE)), 'z', 0, 0)]
    all_gather x1 -> x0, waiting for transfers between devices: 33.9 us -> none  [per_device(): whole = lax.all_gather(fresh, 'shard', axis=0, tiled=True)]
    pallas_call x0 -> x4, Pallas kernels: none -> 7.02 us  [the longest x1 3.45 us: per_device(): pl.pallas_call(update_kernel, out_shape=jax.ShapeDtypeStruct((32, TILE, T...]
    dot_general x6 -> x0, matrix products: 4.72 us -> none  [the longest x1 1.54 us: per_device(): left = jnp.einsum('tik,tkl->til', rows_tab, moment, precision=highest)]
    ppermute x0 -> x1, starting transfers between devices: none -> 3.39 us  [per_device(): other = lax.ppermute(own, 'core', [(0, 1), (1, 0)])]
  transfers between devices with their start and end apart: 1 -> 1, of which waited for: 1 -> 1; matrix products, arithmetic and copies ran while one was open for 1% -> 0% of each run, Pallas kernels for 0% -> 3%
where the time goes in v1:
time: 65.5 us; the launch traced here: 65.2 us
  blocking collectives  49.6 us (76%)
  Pallas kernels  7.02 us (11%)
  local copies, waits for them, and re-layouts  4.33 us (7%)
  starting transfers between devices  3.39 us (5%)
  between operations  0.73 us (1%)
    all_to_all x1, blocking collectives, per_device(): lax.all_to_all(jnp.broadcast_to(packed[None], (16, 8, TILE)), 'z', 0, 0)  27.2 us
    all_to_all x1, blocking collectives, per_device(): own = lax.all_to_all(blocks, PLANE, 0, 0)  22.4 us
    unnamed x17, local copies, waits for them, and re-layouts  4.32 us
    pallas_call x1, Pallas kernels, per_device(): pl.pallas_call(update_kernel, out_shape=jax.ShapeDtypeStruct((32, TILE, T...  3.45 us
    ppermute x1, starting transfers between devices, per_device(): other = lax.ppermute(own, 'core', [(0, 1), (1, 0)])  3.39 us
    pallas_call x1, Pallas kernels, per_device(): pl.pallas_call(momentum_kernel, out_shape=jax.ShapeDtypeStruct((4, TILE,...  1.8 us
  transfers between devices with their start and end apart: 1, of which 1 were waited for; matrix products, arithmetic and copies ran while one was open for 0% of the time, Pallas kernels for 3%

profile of v1, /device:TPU:1, one launch (start us, length us, event | category | flops | bytes accessed | tf_op | source)
XLA Modules:
  0.0 65.2 jit_solution(7834963448078186687)
XLA Ops:
  0.6 0.8 %copy.9.offs_ref = s32[4,2]{1,0:T(4,128)S(1)} copy(s32[4,2]{0,1:T(2,128)} %param.9) | data formatting | bytes 64 | tf_op args[3]
  1.4 0.0 copy-start
  1.4 0.9 %copy-done = f32[1,4,128,128]{3,2,1,0:T(8,128)S(1)} copy-done((f32[1,4,128,128]{3,2,1,0:T(8,128)S(1)}, f32[1,4,128,128]{3,2,1,0:T(8,128)}, u32[]{:S(2)}) %copy-start) | copy-done | bytes 262168
  2.3 0.0 copy-start.2
  2.3 0.8 %copy-done.2 = bf16[256,128]{1,0:T(8,128)(2,1)S(1)} copy-done((bf16[256,128]{1,0:T(8,128)(2,1)S(1)}, bf16[256,128]{1,0:T(8,128)(2,1)}, u32[]{:S(2)}) %copy-start.2) | copy-done | bytes 65560
  3.2 0.0 copy-start.5
  3.2 0.9 %copy-done.5 = bf16[1,4,128,128]{3,2,1,0:T(8,128)(2,1)S(1)} copy-done((bf16[1,4,128,128]{3,2,1,0:T(8,128)(2,1)S(1)}, bf16[1,4,128,128]{3,2,1,0:T(8,128)(2,1)}, u32[]{:S(2)}) %copy-start.5) | copy-done | bytes 131096
  4.1 0.0 copy-start.7
  4.1 0.8 %copy-done.7 = bf16[128,256]{1,0:T(8,128)(2,1)S(1)} copy-done((bf16[128,256]{1,0:T(8,128)(2,1)S(1)}, bf16[128,256]{1,0:T(8,128)(2,1)}, u32[]{:S(2)}) %copy-start.7) | copy-done | bytes 65560
  4.9 1.1 %bands.1 = (f32[8,128]{1,0:T(8,128)S(1)}, f32[16,128]{1,0:T(8,128)S(1)}) custom-call(s32[4,2]{1,0:T(4,128)S(1)} %copy.9.offs_ref, bf16[4,128,128]{2,1,0:T(8,128)(2,1)S(1)} %bitcast.7, f32[4,128,128]{2,1,0:T(8,128)S(1)} %bitcast.4, bf16[128,256]{1,0:T(8,128)(2,1)S(1)} %copy-done.7, bf16[256,128]{1,0:T(8,128)(2,1)S(1)} %copy-done.2), custom_call_target="tpu_custom_call" | custom-call | tf_op jit(solution)/shard_map/bands/pallas_call | solution.py:205
  6.0 0.0 copy-start.4
  6.1 27.2 %all_to_all.10.got_ref = f32[16,8,128]{2,1,0:T(8,128)S(1)} all-to-all(f32[16,8,128]{2,1,0:T(8,128)S(1)} %broadcast_in_dim.10), channel_id=1, replica_groups=mesh['yh'=2,'z'=16,'core'=2,'x'=4,'yl'=2] {'z'}, dimensions={0} | all-to-all | bytes 131072 | tf_op jit(solution)/shard_map/all_to_all | solution.py:213
  33.3 0.0 copy-done.4
  33.3 0.7 %blocks.1 = bf16[32,96,128]{2,1,0:T(8,128)(2,1)S(1)} custom-call(s32[4,2]{1,0:T(4,128)S(1)} %copy.9.offs_ref, f32[16,8,128]{2,1,0:T(8,128)S(1)} %all_to_all.10.got_ref, bf16[8,64,128]{2,1,0:T(8,128)(2,1)S(1)} %bitcast.6), custom_call_target="tpu_custom_call" | custom-call | tf_op jit(solution)/shard_map/blocks/pallas_call | solution.py:214
  34.0 0.0 copy-start.1
  34.0 0.0 copy-start.3
  34.0 0.0 copy-start.6
  34.0 22.4 %all_to_all.11.own_ref = bf16[32,96,128]{2,1,0:T(8,128)(2,1)S(1)} all-to-all(bf16[32,96,128]{2,1,0:T(8,128)(2,1)S(1)} %blocks.1), channel_id=1, replica_groups=mesh['yh'=2,'z'=16,'core'=2,'x'=4,'yl'=2] {'yh','core','x','yl'}, dimensions={0} | all-to-all | bytes 1572864 | tf_op jit(solution)/shard_map/all_to_all | solution.py:222
  56.4 3.4 %collective-permute-start = (bf16[32,96,128]{2,1,0:T(8,128)(2,1)S(1)}, bf16[32,96,128]{2,1,0:T(8,128)(2,1)S(1)}, u32[]{:S(2)}, u32[]{:S(2)}) collective-permute-start(bf16[32,96,128]{2,1,0:T(8,128)(2,1)S(1)} %all_to_all.11.own_ref), channel_id=1, source_target_pairs={{0,8},{8,0},{1,9},{9,1},{2,10},{10,2},{3,11},{11,3},{4,12},{12,4},... | collective-permute-start | bytes 2359304 | tf_op jit(solution)/shard_map/ppermute | solution.py:223
  59.8 0.0 copy-done.1
  59.8 0.0 copy-done.3
  59.8 0.0 copy-done.6
  59.8 1.8 %momentum.1 = f32[4,128,128]{2,1,0:T(8,128)} custom-call(s32[4,2]{1,0:T(4,128)S(1)} %copy.9.offs_ref, bf16[4,128,128]{2,1,0:T(8,128)(2,1)S(1)} %bitcast.8, f32[4,128,128]{2,1,0:T(8,128)S(1)} %bitcast.5, bf16[256,128]{1,0:T(8,128)(2,1)S(1)} %copy-done.3, f32[16,128]{1,0:T(8,128)S(1)} %get-tuple-element.4.bands_ref), custom_call_target="tpu_custom_call" | custom-call | flops 200000000 | bytes 700000 | tf_op jit(solution)/shard_map/momentum/pallas_call | solution.py:224
  61.6 0.1 collective-permute-done.other_ref
  61.7 3.5 %update.1 = bf16[32,128,128]{2,1,0:T(8,128)(2,1)} custom-call(bf16[32,96,128]{2,1,0:T(8,128)(2,1)S(1)} %all_to_all.11.own_ref, bf16[32,96,128]{2,1,0:T(8,128)(2,1)S(1)} %collective-permute-done.other_ref, bf16[256,128]{1,0:T(8,128)(2,1)S(1)} %copy-done.3), custom_call_target="tpu_custom_call" | custom-call | tf_op jit(solution)/shard_map/update/pallas_call | solution.py:233
  (1 shorter events, 0.0 us)
Async XLA Ops:
  1.4 0.9 %copy-start = (f32[1,4,128,128]{3,2,1,0:T(8,128)S(1)}, f32[1,4,128,128]{3,2,1,0:T(8,128)}, u32[]{:S(2)}) copy-start(f32[1,4,128,128]{3,2,1,0:T(8,128)} %param.7) | copy-start | bytes 786436
  2.3 0.8 %copy-start.2 = (bf16[256,128]{1,0:T(8,128)(2,1)S(1)}, bf16[256,128]{1,0:T(8,128)(2,1)}, u32[]{:S(2)}) copy-start(bf16[256,128]{1,0:T(8,128)(2,1)} %constant.5.clone.down_ref) | copy-start | bytes 196612
  3.2 0.9 %copy-start.5 = (bf16[1,4,128,128]{3,2,1,0:T(8,128)(2,1)S(1)}, bf16[1,4,128,128]{3,2,1,0:T(8,128)(2,1)}, u32[]{:S(2)}) copy-start(bf16[1,4,128,128]{3,2,1,0:T(8,128)(2,1)} %param.6) | copy-start | bytes 393220
  4.1 0.8 %copy-start.7 = (bf16[128,256]{1,0:T(8,128)(2,1)S(1)}, bf16[128,256]{1,0:T(8,128)(2,1)}, u32[]{:S(2)}) copy-start(bf16[128,256]{1,0:T(8,128)(2,1)} %constant.4.clone.across_ref) | copy-start | bytes 196612
  6.0 27.3 %copy-start.4 = (bf16[4,128,128]{2,1,0:T(8,128)(2,1)S(1)}, bf16[4,128,128]{2,1,0:T(8,128)(2,1)}, u32[]{:S(2)}) copy-start(bf16[4,128,128]{2,1,0:T(8,128)(2,1)} %param.8) | copy-start | bytes 393220
  34.0 25.8 %copy-start.1 = (f32[1,4,128,128]{3,2,1,0:T(8,128)S(1)}, f32[1,4,128,128]{3,2,1,0:T(8,128)}, u32[]{:S(2)}) copy-start(f32[1,4,128,128]{3,2,1,0:T(8,128)} %param.7) | copy-start | bytes 786436
  34.0 25.8 %copy-start.3 = (bf16[256,128]{1,0:T(8,128)(2,1)S(1)}, bf16[256,128]{1,0:T(8,128)(2,1)}, u32[]{:S(2)}) copy-start(bf16[256,128]{1,0:T(8,128)(2,1)} %constant.5.clone.down_ref) | copy-start | bytes 196612
  34.0 25.8 %copy-start.6 = (bf16[1,4,128,128]{3,2,1,0:T(8,128)(2,1)S(1)}, bf16[1,4,128,128]{3,2,1,0:T(8,128)(2,1)}, u32[]{:S(2)}) copy-start(bf16[1,4,128,128]{3,2,1,0:T(8,128)(2,1)} %param.6) | copy-start | bytes 393220
  56.4 5.3 %collective-permute-start = (bf16[32,96,128]{2,1,0:T(8,128)(2,1)S(1)}, bf16[32,96,128]{2,1,0:T(8,128)(2,1)S(1)}, u32[]{:S(2)}, u32[]{:S(2)}) collective-permute-start(bf16[32,96,128]{2,1,0:T(8,128)(2,1)S(1)} %all_to_all.11.own_ref), channel_id=1, source_target_pairs={{0,8},{8,0},{1,9},{9,1},{2,10},{10,2},{3,11},{11,3},{4,12},{12,4},... | collective-permute-start | bytes 2359304 | tf_op jit(solution)/shard_map/ppermute | solution.py:223

commit v2 on v1

v2 whole, which is shorter than its diff:
```python
import functools
import math

import jax
import jax.numpy as jnp
import numpy as np
from jax import lax
from jax.experimental import pallas as pl
from jax.experimental.pallas import tpu as pltpu
from jax.sharding import Mesh, PartitionSpec as P

BAND = 16
TILE = 128
AXES = ("yh", "z", "core", "x", "yl")
PLANE = ("yh", "x", "yl")
F32 = jnp.float32
BF16 = jnp.bfloat16
ROWS = 160


def cosine_table():
    k = np.arange(TILE, dtype=np.float64)[:, None]
    x = np.arange(TILE, dtype=np.float64)[None, :]
    factor = np.where(k == 0, math.sqrt(1.0 / TILE), math.sqrt(2.0 / TILE))
    return factor * np.cos(math.pi * (x + 0.5) * k / TILE)


def split_table():
    table = cosine_table().astype(np.float32)
    high = table.astype(jnp.bfloat16)
    low = (table - high.astype(np.float32)).astype(jnp.bfloat16)
    return np.concatenate([high.T, low.T], axis=0)


def iota(shape, dim):
    return lax.broadcasted_iota(jnp.int32, shape, dim)


def dot(a, b):
    return lax.dot_general(a, b, (((1,), (0,)), ((), ())), preferred_element_type=F32)


def dot_nt(a, b):
    return lax.dot_general(a, b, (((1,), (1,)), ((), ())), preferred_element_type=F32)


def pieces(v):
    high = v.astype(BF16)
    low = (v - high.astype(F32)).astype(BF16)
    return high, low


def fold(v):
    return v[:, :TILE] + v[:, TILE:]


def wide(v):
    high, low = pieces(v)
    return jnp.concatenate([high, low], axis=1)


def weights(v):
    both = wide(v)
    return jnp.concatenate([both, both], axis=0)


def frequencies(offs_ref, which):
    lane = iota((1, TILE), 1)
    tile = (lane % 64) // BAND
    freq = lane % BAND
    for t in range(4):
        freq = freq + jnp.where(tile == t, offs_ref[which, t], 0)
    return freq


def tables(freq, down):
    picks = (iota((TILE, TILE), 0) == freq).astype(F32).astype(BF16)
    both = dot(down, picks)
    return both[:TILE].astype(BF16), both[TILE:].astype(BF16)


def masks(count, dtype):
    lanes = iota((1, 2 * TILE), 1)
    return [((lanes % TILE) // BAND == t).astype(F32).astype(dtype) for t in range(count)]


def stacked(high, low):
    return jnp.concatenate(
        [jnp.concatenate([high, high], axis=1), jnp.concatenate([low, low], axis=1)], axis=0
    )


def bands_kernel(
    offs_hbm, g_hbm, m_hbm, down_hbm, packed_ref, bands_ref, freq_ref, rows_ref, cols_ref, offs_ref, g_ref, m_ref, down_ref, sems
):
    copies = [
        pltpu.make_async_copy(src, dst, sems.at[i])
        for i, (src, dst) in enumerate(
            ((offs_hbm, offs_ref), (down_hbm, down_ref), (m_hbm, m_ref), (g_hbm, g_ref))
        )
    ]
    for copy in copies:
        copy.start()
    lane = iota((1, TILE), 1)
    slot = (lane % 64) // BAND
    copies[0].wait()
    row_freq, col_freq = frequencies(offs_ref, 0), frequencies(offs_ref, 1)
    steps = iota((BAND, TILE), 1) - iota((BAND, TILE), 0)
    picks = jnp.concatenate([(steps == offs_ref[0, t]).astype(F32) for t in range(4)], axis=0)
    copies[1].wait()
    down = down_ref[...]
    cols_high, cols_low = tables(col_freq, down)
    cols = jnp.concatenate([cols_high, cols_low], axis=1)
    cols_ref[...] = stacked(cols_high, cols_low)
    cols = jnp.concatenate([cols, cols], axis=0)
    rows = dot_nt(picks.astype(BF16), down).astype(BF16)
    rows_ref[...] = jnp.concatenate(tables(row_freq, down), axis=1)
    row = iota((BAND, TILE), 0)
    freq_ref[...] = jnp.where(row == 0, row_freq, col_freq).astype(F32).astype(BF16)
    copies[2].wait()
    copies[3].wait()
    right = jnp.zeros((TILE, TILE), F32)
    for t in range(4):
        moment = 0.9 * m_ref[t] + g_ref[t].astype(F32)
        right = jnp.where(slot == t, fold(dot(wide(moment), cols)), right)
    every = fold(dot(rows, weights(right)))
    bands = jnp.zeros((BAND, TILE), F32)
    for t in range(4):
        bands = jnp.where(slot == t, every[BAND * t : BAND * t + BAND], bands)
    bands_ref[...] = bands
    packed_ref[...] = jnp.where(lane < 64, bands[:8], bands[8:])


def block_kernel(got_ref, params_ref, freq_ref, out_ref):
    first = iota((1, TILE), 1) < 64
    total = jnp.sum(got_ref[...], axis=0)
    turned = pltpu.roll(total, 64, 1)
    high, low = [p.astype(F32) for p in pieces(total)]
    turned_high, turned_low = [p.astype(F32) for p in pieces(turned)]
    bands = jnp.concatenate(
        [jnp.where(first, high, turned_low), jnp.where(first, turned_high, low)], axis=0
    ).astype(BF16)
    block = params_ref[2 * lax.axis_index("core") + lax.axis_index("yh")]
    freq = freq_ref[...]
    for d in range(16):
        out_ref[d, :128] = block
        out_ref[d, 128:144] = bands
        out_ref[d, 144:] = freq


def momentum_kernel(g_ref, m_ref, bands_ref, rows_ref, cols_ref, got_ref, down_ref, out_ref, all_rows_ref, all_cols_ref):
    lane = iota((1, TILE), 1)
    bands = bands_ref[...]
    diagonal = [jnp.where(lane // BAND == t, bands, 0.0) for t in range(4)]
    diagonal = jnp.concatenate(diagonal + [jnp.zeros((64, TILE), F32)], axis=0)
    half = wide(fold(dot(rows_ref[...], weights(diagonal))))
    cols = cols_ref[...]
    for t, mask in enumerate(masks(4, BF16)):
        moment = 0.9 * m_ref[t] + g_ref[t].astype(F32)
        out_ref[t] = moment - fold(dot_nt(half * mask, cols))
    down = down_ref[...]
    for g in range(4):
        freqs = [got_ref[s, 144:160].astype(F32).astype(jnp.int32) for s in (2 * g, 2 * g + 1)]
        freqs = jnp.where(lane < 64, freqs[0], freqs[1])
        all_rows_ref[g] = jnp.concatenate(tables(freqs[0:1], down), axis=1)
        all_cols_ref[g] = stacked(*tables(freqs[1:2], down))


def update_kernel(own_ref, other_ref, rows_ref, cols_ref, out_hbm, out_ref, sems):
    lane = iota((1, TILE), 1)
    first = lane < 64
    core = lax.axis_index("core")
    groups = []
    squares = []
    for g in range(4):
        sums = []
        for s in (2 * g, 2 * g + 1):
            v = sum(ref[i, 128:144].astype(F32) for ref in (own_ref, other_ref) for i in (s, 8 + s))
            sums.append((v + pltpu.roll(v, 64, 1)) * (1.0 / 64))
        groups.append(sums)
        both = jnp.where(first, sums[0], sums[1])
        squares.append(jnp.sum(both * both, axis=0, keepdims=True))
    squares = jnp.concatenate(squares + squares, axis=0)
    same = (iota((TILE, TILE), 0) // BAND == iota((TILE, TILE), 1) // BAND).astype(F32).astype(BF16)
    high, low = pieces(squares)
    mean = (dot(high, same) + dot(low, same)) * (1.0 / (TILE * TILE))
    inverse = 1.0 / jnp.sqrt(mean + 1e-06)
    lanes = (iota((1, 2 * TILE), 1) % TILE) // BAND
    copies = []
    for g in range(4):
        scaled = [v * inverse[g : g + 1] for v in groups[g]]
        diagonal = jnp.concatenate([jnp.where(lane // BAND == t, scaled[t // 4], 0.0) for t in range(8)], axis=0)
        half = wide(fold(dot(rows_ref[g], weights(diagonal))))
        cols = cols_ref[g]
        for ref, half_of in ((own_ref, core), (other_ref, 1 - core)):
            for sh in range(2):
                for yh in range(2):
                    s = 2 * g + sh
                    tile = 2 * half_of + yh
                    mask = (lanes == 4 * sh + tile).astype(F32).astype(BF16)
                    update = fold(dot_nt(half * mask, cols))
                    params = ref[8 * yh + s, :128].astype(F32)
                    out_ref[4 * s + tile] = (params - update).astype(BF16)
        copies.append(
            pltpu.make_async_copy(out_ref.at[pl.ds(8 * g, 8)], out_hbm.at[pl.ds(8 * g, 8)], sems.at[g])
        )
        copies[-1].start()
    for copy in copies:
        copy.wait()


SMEM = pl.BlockSpec(memory_space=pltpu.SMEM)
VMEM = pl.BlockSpec(memory_space=pltpu.VMEM)
HBM = pl.BlockSpec(memory_space=pltpu.HBM)
PARAMS = pltpu.CompilerParams(vmem_limit_bytes=40 * 1024 * 1024)
shape = jax.ShapeDtypeStruct


def per_device(gradients, momentum, params, band_offsets):
    down = jnp.asarray(split_table())
    g, m = gradients[0], momentum[0]
    packed, bands, freq, rows, cols = pl.pallas_call(
        bands_kernel,
        out_shape=(
            shape((8, TILE), F32),
            shape((BAND, TILE), F32),
            shape((BAND, TILE), BF16),
            shape((TILE, 2 * TILE), BF16),
            shape((2 * TILE, 2 * TILE), BF16),
        ),
        in_specs=[HBM] * 4,
        out_specs=(VMEM,) * 5,
        scratch_shapes=[
            pltpu.SMEM((2, 4), jnp.int32),
            pltpu.VMEM((4, TILE, TILE), BF16),
            pltpu.VMEM((4, TILE, TILE), F32),
            pltpu.VMEM((2 * TILE, TILE), BF16),
            pltpu.SemaphoreType.DMA((4,)),
        ],
        compiler_params=pltpu.CompilerParams(vmem_limit_bytes=16 * 1024 * 1024),
        name="bands",
    )(*[pltpu.with_memory_space_constraint(a, pltpu.HBM) for a in (band_offsets.T, g, m, down)])
    got = lax.all_to_all(jnp.broadcast_to(packed[None], (16, 8, TILE)), "z", 0, 0)
    blocks = pl.pallas_call(
        block_kernel,
        out_shape=shape((16, ROWS, TILE), BF16),
        in_specs=[VMEM] * 3,
        out_specs=VMEM,
        compiler_params=PARAMS,
        name="blocks",
    )(got, params, freq)
    own = lax.all_to_all(blocks, PLANE, 0, 0)
    other = lax.ppermute(own, "core", [(0, 1), (1, 0)])
    new_momentum, all_rows, all_cols = pl.pallas_call(
        momentum_kernel,
        out_shape=(
            shape((4, TILE, TILE), F32),
            shape((4, TILE, 2 * TILE), BF16),
            shape((4, 2 * TILE, 2 * TILE), BF16),
        ),
        in_specs=[VMEM] * 7,
        out_specs=(VMEM,) * 3,
        compiler_params=PARAMS,
        cost_estimate=pl.CostEstimate(flops=200_000_000, bytes_accessed=700_000, transcendentals=0),
        name="momentum",
    )(g, m, bands, rows, cols, own, down)
    whole = pl.pallas_call(
        update_kernel,
        out_shape=shape((32, TILE, TILE), BF16),
        in_specs=[VMEM] * 4,
        out_specs=HBM,
        scratch_shapes=[pltpu.VMEM((32, TILE, TILE), BF16), pltpu.SemaphoreType.DMA((4,))],
        compiler_params=PARAMS,
        name="update",
    )(own, other, all_rows, all_cols)
    return (new_momentum[None], whole)


def solution(mesh):
    fine = Mesh(mesh.devices.reshape(2, 16, 2, 4, 2), AXES)
    rep, shard = ("yh", "z", "core"), ("x", "yl")
    in_specs = (P(rep, shard, None, None), P(rep, shard, None, None), P(shard, None, None), P(shard, None))
    out_specs = (P(rep, shard, None, None), P())
    return jax.shard_map(per_device, mesh=fine, in_specs=in_specs, out_specs=out_specs, check_vma=False)
```

time: 65.5 us -> 56.5 us (0.86)
  blocking collectives: 49.6 us -> 44.4 us
  local copies, waits for them, and re-layouts: 4.33 us -> 0.03 us
  starting transfers between devices: 3.39 us -> 5.1 us
  Pallas kernels: 7.02 us -> 5.51 us
    all_to_all x1, blocking collectives: 22.4 us -> 17.2 us  [per_device(): own = lax.all_to_all(blocks, PLANE, 0, 0)]
    unnamed x17 -> x8, local copies, waits for them, and re-layouts: 4.32 us -> 0.02 us
    ppermute x1, starting transfers between devices: 3.39 us -> 5.1 us  [per_device(): other = lax.ppermute(own, 'core', [(0, 1), (1, 0)])]
    pallas_call x4, Pallas kernels: 7.02 us -> 5.51 us  [the longest x1 2.82 us: per_device(): pl.pallas_call(update_kernel, out_shape=shape((32, TILE, TILE), BF16), in...]
  transfers between devices with their start and end apart: 1 -> 1, of which waited for: 1 -> 1; matrix products, arithmetic and copies ran while one was open for 0% -> 0% of each run, Pallas kernels for 3% -> 2%
where the time goes in v2:
time: 56.5 us; the launch traced here: 56.3 us
  blocking collectives  44.4 us (79%)
  Pallas kernels  5.51 us (10%)
  starting transfers between devices  5.1 us (9%)
  between operations  0.71 us (1%)
    all_to_all x1, blocking collectives, per_device(): lax.all_to_all(jnp.broadcast_to(packed[None], (16, 8, TILE)), 'z', 0, 0)  27.2 us
    all_to_all x1, blocking collectives, per_device(): own = lax.all_to_all(blocks, PLANE, 0, 0)  17.2 us
    ppermute x1, starting transfers between devices, per_device(): other = lax.ppermute(own, 'core', [(0, 1), (1, 0)])  5.1 us
    pallas_call x1, Pallas kernels, per_device(): pl.pallas_call(update_kernel, out_shape=shape((32, TILE, TILE), BF16), in...  2.82 us
    pallas_call x1, Pallas kernels, per_device(): pl.pallas_call(bands_kernel, out_shape=(shape((8, TILE), F32), shape((BAN...  1.47 us
  transfers between devices with their start and end apart: 1, of which 1 were waited for; matrix products, arithmetic and copies ran while one was open for 0% of the time, Pallas kernels for 2%

profile of v2, /device:TPU:1, one launch (start us, length us, event | category | flops | bytes accessed | tf_op | source)
XLA Modules:
  0.0 56.3 jit_solution(12896061416814847908)
XLA Ops:
  0.6 1.5 %bands.1 = (f32[8,128]{1,0:T(8,128)S(1)}, f32[16,128]{1,0:T(8,128)S(1)}, bf16[16,128]{1,0:T(8,128)(2,1)S(1)}, bf16[128,256]{1,0:T(8,128)(2,1)S(1)}, bf16[256,256]{1,0:T(8,128)(2,1)S(1)}) custom-call(s32[2,4]{1,0:T(2,128)} %bitcast.8, bf16[4,128,128]{2,1,0:T(8,128)(2,1)} %bitcast.6, f32[4,128,128]{2,1,0:T(8,128)} %bitcast.4, ...), custom_call_target="tpu_custom_call" | custom-call | tf_op jit(solution)/shard_map/bands/pallas_call | solution.py:222
  2.1 0.0 copy-start.3
  2.1 27.2 %all_to_all.10.got_ref = f32[16,8,128]{2,1,0:T(8,128)S(1)} all-to-all(f32[16,8,128]{2,1,0:T(8,128)S(1)} %broadcast_in_dim.4), channel_id=1, replica_groups=mesh['yh'=2,'z'=16,'core'=2,'x'=4,'yl'=2] {'z'}, dimensions={0} | all-to-all | bytes 131072 | tf_op jit(solution)/shard_map/all_to_all | solution.py:243
  29.4 0.0 copy-done.3
  29.4 0.1 blocks.1
  29.5 0.0 copy-start
  29.5 0.0 copy-start.1
  29.5 0.0 copy-start.2
  29.5 17.2 %all_to_all.11.got_ref.own_ref = bf16[16,160,128]{2,1,0:T(8,128)(2,1)S(1)} all-to-all(bf16[16,160,128]{2,1,0:T(8,128)(2,1)S(1)} %blocks.1), channel_id=1, replica_groups=mesh['yh'=2,'z'=16,'core'=2,'x'=4,'yl'=2] {'yh','x','yl'}, dimensions={0} | all-to-all | bytes 1310720 | tf_op jit(solution)/shard_map/all_to_all | solution.py:252
  46.7 5.1 %collective-permute-start = (bf16[16,160,128]{2,1,0:T(8,128)(2,1)S(1)}, bf16[16,160,128]{2,1,0:T(8,128)(2,1)S(1)}, u32[]{:S(2)}, u32[]{:S(2)}) collective-permute-start(bf16[16,160,128]{2,1,0:T(8,128)(2,1)S(1)} %all_to_all.11.got_ref.own_ref), channel_id=1, source_target_pairs={{0,8},{8,0},{1,9},{9,1},{2,10},{10,2},{3,11},{11,3},{4,12},{12,4},... | collective-permute-start | bytes 1966088 | tf_op jit(solution)/shard_map/ppermute | solution.py:253
  51.8 0.0 copy-done
  51.8 0.0 copy-done.1
  51.8 0.0 copy-done.2
  51.8 1.1 %momentum.1 = (f32[4,128,128]{2,1,0:T(8,128)}, bf16[4,128,256]{2,1,0:T(8,128)(2,1)S(1)}, bf16[4,256,256]{2,1,0:T(8,128)(2,1)S(1)}) custom-call(bf16[4,128,128]{2,1,0:T(8,128)(2,1)S(1)} %bitcast.7, f32[4,128,128]{2,1,0:T(8,128)S(1)} %bitcast.5, f32[16,128]{1,0:T(8,128)S(1)} %get-tuple-element.10.bands_ref, bf16[128,256]{1,0:T(8,128)(2,1)S(1)} %get-tuple-element.11.rows_ref, ...), custom_call_target="tpu_custom_call" | custom-call | flops 200000000 | bytes 700000 | tf_op jit(solution)/shard_map/momentum/pallas_call | solution.py:254
  52.9 0.5 collective-permute-done.other_ref
  53.5 2.8 %update.1 = bf16[32,128,128]{2,1,0:T(8,128)(2,1)} custom-call(bf16[16,160,128]{2,1,0:T(8,128)(2,1)S(1)} %all_to_all.11.got_ref.own_ref, bf16[16,160,128]{2,1,0:T(8,128)(2,1)S(1)} %collective-permute-done.other_ref, bf16[4,128,256]{2,1,0:T(8,128)(2,1)S(1)} %get-tuple-element.16.rows_ref, bf16[4,256,256]{2,1,0:T(8,128)(2,1)S(1)} %get-tuple-element.17.cols_ref), custom_call_target="tpu_custom_call" | custom-call | tf_op jit(solution)/shard_map/update/pallas_call | solution.py:267
  (1 shorter events, 0.0 us)
Async XLA Ops:
  2.1 27.3 %copy-start.3 = (bf16[4,128,128]{2,1,0:T(8,128)(2,1)S(1)}, bf16[4,128,128]{2,1,0:T(8,128)(2,1)}, u32[]{:S(2)}) copy-start(bf16[4,128,128]{2,1,0:T(8,128)(2,1)} %params_ref.1) | copy-start | bytes 393220
  29.5 22.3 %copy-start = (f32[1,4,128,128]{3,2,1,0:T(8,128)S(1)}, f32[1,4,128,128]{3,2,1,0:T(8,128)}, u32[]{:S(2)}) copy-start(f32[1,4,128,128]{3,2,1,0:T(8,128)} %param.6) | copy-start | bytes 786436
  29.5 22.3 %copy-start.1 = (bf16[1,4,128,128]{3,2,1,0:T(8,128)(2,1)S(1)}, bf16[1,4,128,128]{3,2,1,0:T(8,128)(2,1)}, u32[]{:S(2)}) copy-start(bf16[1,4,128,128]{3,2,1,0:T(8,128)(2,1)} %param.5) | copy-start | bytes 393220
  29.5 22.3 %copy-start.2 = (bf16[256,128]{1,0:T(8,128)(2,1)S(1)}, bf16[256,128]{1,0:T(8,128)(2,1)}, u32[]{:S(2)}) copy-start(bf16[256,128]{1,0:T(8,128)(2,1)} %constant.2.clone.down_hbm.down_ref) | copy-start | bytes 196612
  46.7 6.8 %collective-permute-start = (bf16[16,160,128]{2,1,0:T(8,128)(2,1)S(1)}, bf16[16,160,128]{2,1,0:T(8,128)(2,1)S(1)}, u32[]{:S(2)}, u32[]{:S(2)}) collective-permute-start(bf16[16,160,128]{2,1,0:T(8,128)(2,1)S(1)} %all_to_all.11.got_ref.own_ref), channel_id=1, source_target_pairs={{0,8},{8,0},{1,9},{9,1},{2,10},{10,2},{3,11},{11,3},{4,12},{12,4},... | collective-permute-start | bytes 1966088 | tf_op jit(solution)/shard_map/ppermute | solution.py:253

commit v3 on v2

--- a/solution.py
+++ b/solution.py
@@ -12,7 +12,7 @@
 BAND = 16
 TILE = 128
 AXES = ("yh", "z", "core", "x", "yl")
-PLANE = ("yh", "x", "yl")
+PLANE = ("yh", "yl", "x")
 F32 = jnp.float32
 BF16 = jnp.bfloat16
 ROWS = 160
@@ -148,6 +148,10 @@
         out_ref[d, 144:] = freq
 
 
+def source(yh, s):
+    return 8 * yh + 4 * (s % 2) + s // 2
+
+
 def momentum_kernel(g_ref, m_ref, bands_ref, rows_ref, cols_ref, got_ref, down_ref, out_ref, all_rows_ref, all_cols_ref):
     lane = iota((1, TILE), 1)
     bands = bands_ref[...]
@@ -160,47 +164,47 @@
         out_ref[t] = moment - fold(dot_nt(half * mask, cols))
     down = down_ref[...]
     for g in range(4):
-        freqs = [got_ref[s, 144:160].astype(F32).astype(jnp.int32) for s in (2 * g, 2 * g + 1)]
+        freqs = [got_ref[source(0, s), 144:160].astype(F32).astype(jnp.int32) for s in (2 * g, 2 * g + 1)]
         freqs = jnp.where(lane < 64, freqs[0], freqs[1])
         all_rows_ref[g] = jnp.concatenate(tables(freqs[0:1], down), axis=1)
-        all_cols_ref[g] = stacked(*tables(freqs[1:2], down))
+        picks = (iota((TILE, TILE), 0) == freqs[1:2]).astype(F32).T.astype(BF16)
+        all_cols_ref[g] = dot_nt(picks, down).astype(BF16)
 
 
 def update_kernel(own_ref, other_ref, rows_ref, cols_ref, out_hbm, out_ref, sems):
     lane = iota((1, TILE), 1)
     first = lane < 64
     core = lax.axis_index("core")
-    groups = []
+    halves = []
     squares = []
     for g in range(4):
         sums = []
         for s in (2 * g, 2 * g + 1):
-            v = sum(ref[i, 128:144].astype(F32) for ref in (own_ref, other_ref) for i in (s, 8 + s))
+            v = sum(ref[source(yh, s), 128:144].astype(F32) for ref in (own_ref, other_ref) for yh in range(2))
             sums.append((v + pltpu.roll(v, 64, 1)) * (1.0 / 64))
-        groups.append(sums)
         both = jnp.where(first, sums[0], sums[1])
         squares.append(jnp.sum(both * both, axis=0, keepdims=True))
+        diagonal = jnp.concatenate([jnp.where(lane // BAND == t, sums[t // 4], 0.0) for t in range(8)], axis=0)
+        halves.append(fold(dot(rows_ref[g], weights(diagonal))))
     squares = jnp.concatenate(squares + squares, axis=0)
     same = (iota((TILE, TILE), 0) // BAND == iota((TILE, TILE), 1) // BAND).astype(F32).astype(BF16)
     high, low = pieces(squares)
     mean = (dot(high, same) + dot(low, same)) * (1.0 / (TILE * TILE))
     inverse = 1.0 / jnp.sqrt(mean + 1e-06)
     lanes = (iota((1, 2 * TILE), 1) % TILE) // BAND
+    order = [(ref, half_of, sh, yh) for ref, half_of in ((own_ref, core), (other_ref, 1 - core)) for sh in range(2) for yh in range(2)]
     copies = []
     for g in range(4):
-        scaled = [v * inverse[g : g + 1] for v in groups[g]]
-        diagonal = jnp.concatenate([jnp.where(lane // BAND == t, scaled[t // 4], 0.0) for t in range(8)], axis=0)
-        half = wide(fold(dot(rows_ref[g], weights(diagonal))))
+        half = wide(halves[g] * inverse[g : g + 1])
+        left = jnp.concatenate(
+            [half * (lanes == 4 * sh + 2 * half_of + yh).astype(F32).astype(BF16) for _, half_of, sh, yh in order], axis=0
+        )
         cols = cols_ref[g]
-        for ref, half_of in ((own_ref, core), (other_ref, 1 - core)):
-            for sh in range(2):
-                for yh in range(2):
-                    s = 2 * g + sh
-                    tile = 2 * half_of + yh
-                    mask = (lanes == 4 * sh + tile).astype(F32).astype(BF16)
-                    update = fold(dot_nt(half * mask, cols))
-                    params = ref[8 * yh + s, :128].astype(F32)
-                    out_ref[4 * s + tile] = (params - update).astype(BF16)
+        update = fold(dot(left, jnp.concatenate([cols, cols], axis=0)))
+        for i, (ref, half_of, sh, yh) in enumerate(order):
+            s = 2 * g + sh
+            params = ref[source(yh, s), :128].astype(F32)
+            out_ref[4 * s + 2 * half_of + yh] = (params - update[TILE * i : TILE * i + TILE]).astype(BF16)
         copies.append(
             pltpu.make_async_copy(out_ref.at[pl.ds(8 * g, 8)], out_hbm.at[pl.ds(8 * g, 8)], sems.at[g])
         )
@@ -256,7 +260,7 @@
         out_shape=(
             shape((4, TILE, TILE), F32),
             shape((4, TILE, 2 * TILE), BF16),
-            shape((4, 2 * TILE, 2 * TILE), BF16),
+            shape((4, TILE, 2 * TILE), BF16),
         ),
         in_specs=[VMEM] * 7,
         out_specs=(VMEM,) * 3,

time: 56.5 us -> 55.8 us (0.988)
  Pallas kernels: 5.51 us -> 4.62 us
    pallas_call x1, Pallas kernels: 2.82 us -> 1.91 us  [per_device(): pl.pallas_call(update_kernel, out_shape=shape((32, TILE, TILE), BF16), in...]
where the time goes in v3:
time: 55.8 us; the launch traced here: 55.6 us
  blocking collectives  44.6 us (80%)
  starting transfers between devices  5.12 us (9%)
  Pallas kernels  4.62 us (8%)
  between operations  0.71 us (1%)
    all_to_all x1, blocking collectives, per_device(): lax.all_to_all(jnp.broadcast_to(packed[None], (16, 8, TILE)), 'z', 0, 0)  27.2 us
    all_to_all x1, blocking collectives, per_device(): own = lax.all_to_all(blocks, PLANE, 0, 0)  17.4 us
    ppermute x1, starting transfers between devices, per_device(): other = lax.ppermute(own, 'core', [(0, 1), (1, 0)])  5.12 us
    pallas_call x1, Pallas kernels, per_device(): pl.pallas_call(update_kernel, out_shape=shape((32, TILE, TILE), BF16), in...  1.91 us
    pallas_call x1, Pallas kernels, per_device(): pl.pallas_call(bands_kernel, out_shape=(shape((8, TILE), F32), shape((BAN...  1.47 us
    pallas_call x1, Pallas kernels, per_device(): pl.pallas_call(momentum_kernel, out_shape=(shape((4, TILE, TILE), F32), s...  1.14 us
  transfers between devices with their start and end apart: 1, of which 1 were waited for; matrix products, arithmetic and copies ran while one was open for 0% of the time, Pallas kernels for 2%

profile of v3, /device:TPU:1, one launch (start us, length us, event | category | flops | bytes accessed | tf_op | source)
XLA Modules:
  0.0 55.6 jit_solution(10109743257403882058)
XLA Ops:
  0.6 1.5 %bands.1 = (f32[8,128]{1,0:T(8,128)S(1)}, f32[16,128]{1,0:T(8,128)S(1)}, bf16[16,128]{1,0:T(8,128)(2,1)S(1)}, bf16[128,256]{1,0:T(8,128)(2,1)S(1)}, bf16[256,256]{1,0:T(8,128)(2,1)S(1)}) custom-call(s32[2,4]{1,0:T(2,128)} %bitcast.8, bf16[4,128,128]{2,1,0:T(8,128)(2,1)} %bitcast.6, f32[4,128,128]{2,1,0:T(8,128)} %bitcast.4, ...), custom_call_target="tpu_custom_call" | custom-call | tf_op jit(solution)/shard_map/bands/pallas_call | solution.py:226
  2.1 0.0 copy-start.3
  2.1 27.2 %all_to_all.10.got_ref = f32[16,8,128]{2,1,0:T(8,128)S(1)} all-to-all(f32[16,8,128]{2,1,0:T(8,128)S(1)} %broadcast_in_dim.4), channel_id=1, replica_groups=mesh['yh'=2,'z'=16,'core'=2,'x'=4,'yl'=2] {'z'}, dimensions={0} | all-to-all | bytes 131072 | tf_op jit(solution)/shard_map/all_to_all | solution.py:247
  29.4 0.0 copy-done.3
  29.4 0.1 blocks.1
  29.5 0.0 copy-start
  29.5 0.0 copy-start.1
  29.5 0.0 copy-start.2
  29.5 17.4 %all_to_all.11.got_ref.own_ref = bf16[16,160,128]{2,1,0:T(8,128)(2,1)S(1)} all-to-all(bf16[16,160,128]{2,1,0:T(8,128)(2,1)S(1)} %blocks.1), channel_id=1, replica_groups=mesh['yh'=2,'z'=16,'core'=2,'x'=4,'yl'=2] {'yh','yl','x'}, dimensions={0} | all-to-all | bytes 1310720 | tf_op jit(solution)/shard_map/all_to_all | solution.py:256
  46.9 5.1 %collective-permute-start = (bf16[16,160,128]{2,1,0:T(8,128)(2,1)S(1)}, bf16[16,160,128]{2,1,0:T(8,128)(2,1)S(1)}, u32[]{:S(2)}, u32[]{:S(2)}) collective-permute-start(bf16[16,160,128]{2,1,0:T(8,128)(2,1)S(1)} %all_to_all.11.got_ref.own_ref), channel_id=1, source_target_pairs={{0,8},{8,0},{1,9},{9,1},{2,10},{10,2},{3,11},{11,3},{4,12},{12,4},... | collective-permute-start | bytes 1966088 | tf_op jit(solution)/shard_map/ppermute | solution.py:257
  52.0 0.0 copy-done
  52.0 0.0 copy-done.1
  52.0 0.0 copy-done.2
  52.0 1.1 %momentum.1 = (f32[4,128,128]{2,1,0:T(8,128)}, bf16[4,128,256]{2,1,0:T(8,128)(2,1)S(1)}, bf16[4,128,256]{2,1,0:T(8,128)(2,1)S(1)}) custom-call(bf16[4,128,128]{2,1,0:T(8,128)(2,1)S(1)} %bitcast.7, f32[4,128,128]{2,1,0:T(8,128)S(1)} %bitcast.5, f32[16,128]{1,0:T(8,128)S(1)} %get-tuple-element.10.bands_ref, bf16[128,256]{1,0:T(8,128)(2,1)S(1)} %get-tuple-element.11.rows_ref, ...), custom_call_target="tpu_custom_call" | custom-call | flops 200000000 | bytes 700000 | tf_op jit(solution)/shard_map/momentum/pallas_call | solution.py:258
  53.2 0.5 collective-permute-done.other_ref
  53.7 1.9 %update.1 = bf16[32,128,128]{2,1,0:T(8,128)(2,1)} custom-call(bf16[16,160,128]{2,1,0:T(8,128)(2,1)S(1)} %all_to_all.11.got_ref.own_ref, bf16[16,160,128]{2,1,0:T(8,128)(2,1)S(1)} %collective-permute-done.other_ref, bf16[4,128,256]{2,1,0:T(8,128)(2,1)S(1)} %get-tuple-element.16.rows_ref, bf16[4,128,256]{2,1,0:T(8,128)(2,1)S(1)} %get-tuple-element.17.cols_ref), custom_call_target="tpu_custom_call" | custom-call | tf_op jit(solution)/shard_map/update/pallas_call | solution.py:271
  (1 shorter events, 0.0 us)
Async XLA Ops:
  2.1 27.3 %copy-start.3 = (bf16[4,128,128]{2,1,0:T(8,128)(2,1)S(1)}, bf16[4,128,128]{2,1,0:T(8,128)(2,1)}, u32[]{:S(2)}) copy-start(bf16[4,128,128]{2,1,0:T(8,128)(2,1)} %params_ref.1) | copy-start | bytes 393220
  29.5 22.5 %copy-start = (f32[1,4,128,128]{3,2,1,0:T(8,128)S(1)}, f32[1,4,128,128]{3,2,1,0:T(8,128)}, u32[]{:S(2)}) copy-start(f32[1,4,128,128]{3,2,1,0:T(8,128)} %param.6) | copy-start | bytes 786436
  29.5 22.5 %copy-start.1 = (bf16[1,4,128,128]{3,2,1,0:T(8,128)(2,1)S(1)}, bf16[1,4,128,128]{3,2,1,0:T(8,128)(2,1)}, u32[]{:S(2)}) copy-start(bf16[1,4,128,128]{3,2,1,0:T(8,128)(2,1)} %param.5) | copy-start | bytes 393220
  29.5 22.5 %copy-start.2 = (bf16[256,128]{1,0:T(8,128)(2,1)S(1)}, bf16[256,128]{1,0:T(8,128)(2,1)}, u32[]{:S(2)}) copy-start(bf16[256,128]{1,0:T(8,128)(2,1)} %constant.2.clone.down_hbm.down_ref) | copy-start | bytes 196612
  46.9 6.8 %collective-permute-start = (bf16[16,160,128]{2,1,0:T(8,128)(2,1)S(1)}, bf16[16,160,128]{2,1,0:T(8,128)(2,1)S(1)}, u32[]{:S(2)}, u32[]{:S(2)}) collective-permute-start(bf16[16,160,128]{2,1,0:T(8,128)(2,1)S(1)} %all_to_all.11.got_ref.own_ref), channel_id=1, source_target_pairs={{0,8},{8,0},{1,9},{9,1},{2,10},{10,2},{3,11},{11,3},{4,12},{12,4},... | collective-permute-start | bytes 1966088 | tf_op jit(solution)/shard_map/ppermute | solution.py:257

commit v4 on v3

--- a/solution.py
+++ b/solution.py
@@ -149,7 +149,7 @@
 
 
 def source(yh, s):
-    return 8 * yh + 4 * (s % 2) + s // 2
+    return 15 - (8 * yh + 4 * (s % 2) + s // 2)
 
 
 def momentum_kernel(g_ref, m_ref, bands_ref, rows_ref, cols_ref, got_ref, down_ref, out_ref, all_rows_ref, all_cols_ref):
@@ -244,7 +244,7 @@
         compiler_params=pltpu.CompilerParams(vmem_limit_bytes=16 * 1024 * 1024),
         name="bands",
     )(*[pltpu.with_memory_space_constraint(a, pltpu.HBM) for a in (band_offsets.T, g, m, down)])
-    got = lax.all_to_all(jnp.broadcast_to(packed[None], (16, 8, TILE)), "z", 0, 0)
+    got = lax.all_to_all(jnp.broadcast_to(packed[None], (16, 8, TILE)), "z", 0, 0, axis_index_groups=[[(z + 8) % 16 for z in range(16)]])
     blocks = pl.pallas_call(
         block_kernel,
         out_shape=shape((16, ROWS, TILE), BF16),
@@ -253,7 +253,7 @@
         compiler_params=PARAMS,
         name="blocks",
     )(got, params, freq)
-    own = lax.all_to_all(blocks, PLANE, 0, 0)
+    own = lax.all_to_all(blocks, PLANE, 0, 0, axis_index_groups=[list(range(15, -1, -1))])
     other = lax.ppermute(own, "core", [(0, 1), (1, 0)])
     new_momentum, all_rows, all_cols = pl.pallas_call(
         momentum_kernel,

time: 55.8 us -> 48.8 us (0.87)
  blocking collectives: 44.6 us -> 37.6 us
    all_to_all x2, blocking collectives: 44.6 us -> 37.6 us  [the longest x1 22.3 us: per_device(): lax.all_to_all(jnp.broadcast_to(packed[None], (16, 8, TILE)), 'z', 0, 0,...]
where the time goes in v4:
time: 48.8 us; the launch traced here: 48.5 us
  blocking collectives  37.6 us (77%)
  starting transfers between devices  5.08 us (10%)
  Pallas kernels  4.62 us (9%)
  between operations  0.71 us (1%)
  waiting for transfers between devices  0.53 us (1%)
    all_to_all x1, blocking collectives, per_device(): lax.all_to_all(jnp.broadcast_to(packed[None], (16, 8, TILE)), 'z', 0, 0,...  22.3 us
    all_to_all x1, blocking collectives, per_device(): lax.all_to_all(blocks, PLANE, 0, 0, axis_index_groups=[list(range(15, -1,...  15.3 us
    ppermute x1, starting transfers between devices, per_device(): other = lax.ppermute(own, 'core', [(0, 1), (1, 0)])  5.08 us
    pallas_call x1, Pallas kernels, per_device(): pl.pallas_call(update_kernel, out_shape=shape((32, TILE, TILE), BF16), in...  1.91 us
    pallas_call x1, Pallas kernels, per_device(): pl.pallas_call(bands_kernel, out_shape=(shape((8, TILE), F32), shape((BAN...  1.47 us
    pallas_call x1, Pallas kernels, per_device(): pl.pallas_call(momentum_kernel, out_shape=(shape((4, TILE, TILE), F32), s...  1.14 us
  transfers between devices with their start and end apart: 1, of which 1 were waited for; matrix products, arithmetic and copies ran while one was open for 0% of the time, Pallas kernels for 2%

profile of v4, /device:TPU:1, one launch (start us, length us, event | category | flops | bytes accessed | tf_op | source)
XLA Modules:
  0.0 48.5 jit_solution(4608579636191413561)
XLA Ops:
  0.6 1.5 %bands.1 = (f32[8,128]{1,0:T(8,128)S(1)}, f32[16,128]{1,0:T(8,128)S(1)}, bf16[16,128]{1,0:T(8,128)(2,1)S(1)}, bf16[128,256]{1,0:T(8,128)(2,1)S(1)}, bf16[256,256]{1,0:T(8,128)(2,1)S(1)}) custom-call(s32[2,4]{1,0:T(2,128)} %bitcast.8, bf16[4,128,128]{2,1,0:T(8,128)(2,1)} %bitcast.6, f32[4,128,128]{2,1,0:T(8,128)} %bitcast.4, ...), custom_call_target="tpu_custom_call" | custom-call | tf_op jit(solution)/shard_map/bands/pallas_call | solution.py:226
  2.1 0.0 copy-start.3
  2.1 22.3 %all_to_all.10.got_ref = f32[16,8,128]{2,1,0:T(8,128)S(1)} all-to-all(f32[16,8,128]{2,1,0:T(8,128)S(1)} %broadcast_in_dim.4), channel_id=1, replica_groups={{128,144,160,176,192,208,224,240,0,16,32,48,64,80,96,112},{129,145,161,..., dimensions={0} | all-to-all | bytes 131072 | tf_op jit(solution)/shard_map/all_to_all | solution.py:247
  24.4 0.0 copy-done.3
  24.5 0.1 blocks.1
  24.5 0.0 copy-start
  24.6 0.0 copy-start.1
  24.6 0.0 copy-start.2
  24.6 15.3 %all_to_all.11.got_ref.own_ref = bf16[16,160,128]{2,1,0:T(8,128)(2,1)S(1)} all-to-all(bf16[16,160,128]{2,1,0:T(8,128)(2,1)S(1)} %blocks.1), channel_id=1, replica_groups={{263,261,259,257,262,260,258,256,7,5,3,1,6,4,2,0},{271,269,267,265,270,..., dimensions={0} | all-to-all | bytes 1310720 | tf_op jit(solution)/shard_map/all_to_all | solution.py:256
  39.9 5.1 %collective-permute-start = (bf16[16,160,128]{2,1,0:T(8,128)(2,1)S(1)}, bf16[16,160,128]{2,1,0:T(8,128)(2,1)S(1)}, u32[]{:S(2)}, u32[]{:S(2)}) collective-permute-start(bf16[16,160,128]{2,1,0:T(8,128)(2,1)S(1)} %all_to_all.11.got_ref.own_ref), channel_id=1, source_target_pairs={{0,8},{8,0},{1,9},{9,1},{2,10},{10,2},{3,11},{11,3},{4,12},{12,4},... | collective-permute-start | bytes 1966088 | tf_op jit(solution)/shard_map/ppermute | solution.py:257
  44.9 0.0 copy-done
  44.9 0.0 copy-done.1
  45.0 0.0 copy-done.2
  45.0 1.1 %momentum.1 = (f32[4,128,128]{2,1,0:T(8,128)}, bf16[4,128,256]{2,1,0:T(8,128)(2,1)S(1)}, bf16[4,128,256]{2,1,0:T(8,128)(2,1)S(1)}) custom-call(bf16[4,128,128]{2,1,0:T(8,128)(2,1)S(1)} %bitcast.7, f32[4,128,128]{2,1,0:T(8,128)S(1)} %bitcast.5, f32[16,128]{1,0:T(8,128)S(1)} %get-tuple-element.10.bands_ref, bf16[128,256]{1,0:T(8,128)(2,1)S(1)} %get-tuple-element.11.rows_ref, ...), custom_call_target="tpu_custom_call" | custom-call | flops 200000000 | bytes 700000 | tf_op jit(solution)/shard_map/momentum/pallas_call | solution.py:258
  46.1 0.5 %collective-permute-done.other_ref = bf16[16,160,128]{2,1,0:T(8,128)(2,1)S(1)} collective-permute-done((bf16[16,160,128]{2,1,0:T(8,128)(2,1)S(1)}, bf16[16,160,128]{2,1,0:T(8,128)(2,1)S(1)}, u32[]{:S(2)}, u32[]{:S(2)}) %collective-permute-start) | collective-permute-done | bytes 655392 | tf_op jit(solution)/shard_map/ppermute | solution.py:257
  46.6 1.9 %update.1 = bf16[32,128,128]{2,1,0:T(8,128)(2,1)} custom-call(bf16[16,160,128]{2,1,0:T(8,128)(2,1)S(1)} %all_to_all.11.got_ref.own_ref, bf16[16,160,128]{2,1,0:T(8,128)(2,1)S(1)} %collective-permute-done.other_ref, bf16[4,128,256]{2,1,0:T(8,128)(2,1)S(1)} %get-tuple-element.16.rows_ref, bf16[4,128,256]{2,1,0:T(8,128)(2,1)S(1)} %get-tuple-element.17.cols_ref), custom_call_target="tpu_custom_call" | custom-call | tf_op jit(solution)/shard_map/update/pallas_call | solution.py:271
  (1 shorter events, 0.0 us)
Async XLA Ops:
  2.1 22.3 %copy-start.3 = (bf16[4,128,128]{2,1,0:T(8,128)(2,1)S(1)}, bf16[4,128,128]{2,1,0:T(8,128)(2,1)}, u32[]{:S(2)}) copy-start(bf16[4,128,128]{2,1,0:T(8,128)(2,1)} %params_ref.1) | copy-start | bytes 393220
  24.5 20.4 %copy-start = (f32[1,4,128,128]{3,2,1,0:T(8,128)S(1)}, f32[1,4,128,128]{3,2,1,0:T(8,128)}, u32[]{:S(2)}) copy-start(f32[1,4,128,128]{3,2,1,0:T(8,128)} %param.6) | copy-start | bytes 786436
  24.6 20.4 %copy-start.1 = (bf16[1,4,128,128]{3,2,1,0:T(8,128)(2,1)S(1)}, bf16[1,4,128,128]{3,2,1,0:T(8,128)(2,1)}, u32[]{:S(2)}) copy-start(bf16[1,4,128,128]{3,2,1,0:T(8,128)(2,1)} %param.5) | copy-start | bytes 393220
  24.6 20.4 %copy-start.2 = (bf16[256,128]{1,0:T(8,128)(2,1)S(1)}, bf16[256,128]{1,0:T(8,128)(2,1)}, u32[]{:S(2)}) copy-start(bf16[256,128]{1,0:T(8,128)(2,1)} %constant.2.clone.down_hbm.down_ref) | copy-start | bytes 196612
  39.9 6.8 %collective-permute-start = (bf16[16,160,128]{2,1,0:T(8,128)(2,1)S(1)}, bf16[16,160,128]{2,1,0:T(8,128)(2,1)S(1)}, u32[]{:S(2)}, u32[]{:S(2)}) collective-permute-start(bf16[16,160,128]{2,1,0:T(8,128)(2,1)S(1)} %all_to_all.11.got_ref.own_ref), channel_id=1, source_target_pairs={{0,8},{8,0},{1,9},{9,1},{2,10},{10,2},{3,11},{11,3},{4,12},{12,4},... | collective-permute-start | bytes 1966088 | tf_op jit(solution)/shard_map/ppermute | solution.py:257

commit v5 on v4

--- a/solution.py
+++ b/solution.py
@@ -15,6 +15,8 @@
 PLANE = ("yh", "yl", "x")
 F32 = jnp.float32
 BF16 = jnp.bfloat16
+Z_ORDER = [(z + 9) % 16 for z in range(16)]
+PLANE_ORDER = [10] + [i for i in range(15, -1, -1) if i != 10]
 ROWS = 160
 
 
@@ -149,7 +151,7 @@
 
 
 def source(yh, s):
-    return 15 - (8 * yh + 4 * (s % 2) + s // 2)
+    return PLANE_ORDER.index(8 * yh + 4 * (s % 2) + s // 2)
 
 
 def momentum_kernel(g_ref, m_ref, bands_ref, rows_ref, cols_ref, got_ref, down_ref, out_ref, all_rows_ref, all_cols_ref):
@@ -192,7 +194,7 @@
     mean = (dot(high, same) + dot(low, same)) * (1.0 / (TILE * TILE))
     inverse = 1.0 / jnp.sqrt(mean + 1e-06)
     lanes = (iota((1, 2 * TILE), 1) % TILE) // BAND
-    order = [(ref, half_of, sh, yh) for ref, half_of in ((own_ref, core), (other_ref, 1 - core)) for sh in range(2) for yh in range(2)]
+    order = [(ref, half_of, sh, yh) for sh in range(2) for ref, half_of in ((own_ref, core), (other_ref, 1 - core)) for yh in range(2)]
     copies = []
     for g in range(4):
         half = wide(halves[g] * inverse[g : g + 1])
@@ -205,10 +207,10 @@
             s = 2 * g + sh
             params = ref[source(yh, s), :128].astype(F32)
             out_ref[4 * s + 2 * half_of + yh] = (params - update[TILE * i : TILE * i + TILE]).astype(BF16)
-        copies.append(
-            pltpu.make_async_copy(out_ref.at[pl.ds(8 * g, 8)], out_hbm.at[pl.ds(8 * g, 8)], sems.at[g])
-        )
-        copies[-1].start()
+            if i % 4 == 3:
+                tiles = pl.ds(4 * s, 4)
+                copies.append(pltpu.make_async_copy(out_ref.at[tiles], out_hbm.at[tiles], sems.at[s]))
+                copies[-1].start()
     for copy in copies:
         copy.wait()
 
@@ -244,7 +246,7 @@
         compiler_params=pltpu.CompilerParams(vmem_limit_bytes=16 * 1024 * 1024),
         name="bands",
     )(*[pltpu.with_memory_space_constraint(a, pltpu.HBM) for a in (band_offsets.T, g, m, down)])
-    got = lax.all_to_all(jnp.broadcast_to(packed[None], (16, 8, TILE)), "z", 0, 0, axis_index_groups=[[(z + 8) % 16 for z in range(16)]])
+    got = lax.all_to_all(jnp.broadcast_to(packed[None], (16, 8, TILE)), "z", 0, 0, axis_index_groups=[Z_ORDER])
     blocks = pl.pallas_call(
         block_kernel,
         out_shape=shape((16, ROWS, TILE), BF16),
@@ -253,7 +255,7 @@
         compiler_params=PARAMS,
         name="blocks",
     )(got, params, freq)
-    own = lax.all_to_all(blocks, PLANE, 0, 0, axis_index_groups=[list(range(15, -1, -1))])
+    own = lax.all_to_all(blocks, PLANE, 0, 0, axis_index_groups=[PLANE_ORDER])
     other = lax.ppermute(own, "core", [(0, 1), (1, 0)])
     new_momentum, all_rows, all_cols = pl.pallas_call(
         momentum_kernel,
@@ -273,7 +275,7 @@
         out_shape=shape((32, TILE, TILE), BF16),
         in_specs=[VMEM] * 4,
         out_specs=HBM,
-        scratch_shapes=[pltpu.VMEM((32, TILE, TILE), BF16), pltpu.SemaphoreType.DMA((4,))],
+        scratch_shapes=[pltpu.VMEM((32, TILE, TILE), BF16), pltpu.SemaphoreType.DMA((8,))],
         compiler_params=PARAMS,
         name="update",
     )(own, other, all_rows, all_cols)

time: 48.8 us -> 47.6 us (0.975)
  blocking collectives: 37.6 us -> 36.7 us
    all_to_all x1, blocking collectives: 15.3 us -> 14.5 us  [per_device(): own = lax.all_to_all(blocks, PLANE, 0, 0, axis_index_groups=[PLANE_ORDER])]
where the time goes in v5:
time: 47.6 us; the launch traced here: 47.4 us
  blocking collectives  36.7 us (77%)
  starting transfers between devices  4.78 us (10%)
  Pallas kernels  4.6 us (10%)
  between operations  0.71 us (1%)
  waiting for transfers between devices  0.53 us (1%)
    all_to_all x1, blocking collectives, per_device(): lax.all_to_all(jnp.broadcast_to(packed[None], (16, 8, TILE)), 'z', 0, 0,...  22.2 us
    all_to_all x1, blocking collectives, per_device(): own = lax.all_to_all(blocks, PLANE, 0, 0, axis_index_groups=[PLANE_ORDER])  14.5 us
    ppermute x1, starting transfers between devices, per_device(): other = lax.ppermute(own, 'core', [(0, 1), (1, 0)])  4.78 us
    pallas_call x1, Pallas kernels, per_device(): pl.pallas_call(update_kernel, out_shape=shape((32, TILE, TILE), BF16), in...  1.89 us
    pallas_call x1, Pallas kernels, per_device(): pl.pallas_call(bands_kernel, out_shape=(shape((8, TILE), F32), shape((BAN...  1.47 us
    pallas_call x1, Pallas kernels, per_device(): pl.pallas_call(momentum_kernel, out_shape=(shape((4, TILE, TILE), F32), s...  1.14 us
  transfers between devices with their start and end apart: 1, of which 1 were waited for; matrix products, arithmetic and copies ran while one was open for 0% of the time, Pallas kernels for 2%

profile of v5, /device:TPU:1, one launch (start us, length us, event | category | flops | bytes accessed | tf_op | source)
XLA Modules:
  0.0 47.4 jit_solution(18209281614833178968)
XLA Ops:
  0.6 1.5 %bands.1 = (f32[8,128]{1,0:T(8,128)S(1)}, f32[16,128]{1,0:T(8,128)S(1)}, bf16[16,128]{1,0:T(8,128)(2,1)S(1)}, bf16[128,256]{1,0:T(8,128)(2,1)S(1)}, bf16[256,256]{1,0:T(8,128)(2,1)S(1)}) custom-call(s32[2,4]{1,0:T(2,128)} %bitcast.8, bf16[4,128,128]{2,1,0:T(8,128)(2,1)} %bitcast.6, f32[4,128,128]{2,1,0:T(8,128)} %bitcast.4, ...), custom_call_target="tpu_custom_call" | custom-call | tf_op jit(solution)/shard_map/bands/pallas_call | solution.py:228
  2.1 0.0 copy-start.3
  2.1 22.2 %all_to_all.10.got_ref = f32[16,8,128]{2,1,0:T(8,128)S(1)} all-to-all(f32[16,8,128]{2,1,0:T(8,128)S(1)} %broadcast_in_dim.4), channel_id=1, replica_groups={{144,160,176,192,208,224,240,0,16,32,48,64,80,96,112,128},{145,161,177,..., dimensions={0} | all-to-all | bytes 131072 | tf_op jit(solution)/shard_map/all_to_all | solution.py:249
  24.3 0.0 copy-done.3
  24.3 0.1 blocks.1
  24.4 0.0 copy-start
  24.4 0.0 copy-start.1
  24.4 0.0 copy-start.2
  24.4 14.5 %all_to_all.11.got_ref.own_ref = bf16[16,160,128]{2,1,0:T(8,128)(2,1)S(1)} all-to-all(bf16[16,160,128]{2,1,0:T(8,128)(2,1)S(1)} %blocks.1), channel_id=1, replica_groups={{260,263,261,259,257,262,258,256,7,5,3,1,6,4,2,0},{268,271,269,267,265,..., dimensions={0} | all-to-all | bytes 1310720 | tf_op jit(solution)/shard_map/all_to_all | solution.py:258
  39.0 4.8 %collective-permute-start = (bf16[16,160,128]{2,1,0:T(8,128)(2,1)S(1)}, bf16[16,160,128]{2,1,0:T(8,128)(2,1)S(1)}, u32[]{:S(2)}, u32[]{:S(2)}) collective-permute-start(bf16[16,160,128]{2,1,0:T(8,128)(2,1)S(1)} %all_to_all.11.got_ref.own_ref), channel_id=1, source_target_pairs={{0,8},{8,0},{1,9},{9,1},{2,10},{10,2},{3,11},{11,3},{4,12},{12,4},... | collective-permute-start | bytes 1966088 | tf_op jit(solution)/shard_map/ppermute | solution.py:259
  43.8 0.0 copy-done
  43.8 0.0 copy-done.1
  43.8 0.0 copy-done.2
  43.8 1.1 %momentum.1 = (f32[4,128,128]{2,1,0:T(8,128)}, bf16[4,128,256]{2,1,0:T(8,128)(2,1)S(1)}, bf16[4,128,256]{2,1,0:T(8,128)(2,1)S(1)}) custom-call(bf16[4,128,128]{2,1,0:T(8,128)(2,1)S(1)} %bitcast.7, f32[4,128,128]{2,1,0:T(8,128)S(1)} %bitcast.5, f32[16,128]{1,0:T(8,128)S(1)} %get-tuple-element.10.bands_ref, bf16[128,256]{1,0:T(8,128)(2,1)S(1)} %get-tuple-element.11.rows_ref, ...), custom_call_target="tpu_custom_call" | custom-call | flops 200000000 | bytes 700000 | tf_op jit(solution)/shard_map/momentum/pallas_call | solution.py:260
  45.0 0.5 %collective-permute-done.other_ref = bf16[16,160,128]{2,1,0:T(8,128)(2,1)S(1)} collective-permute-done((bf16[16,160,128]{2,1,0:T(8,128)(2,1)S(1)}, bf16[16,160,128]{2,1,0:T(8,128)(2,1)S(1)}, u32[]{:S(2)}, u32[]{:S(2)}) %collective-permute-start) | collective-permute-done | bytes 655392 | tf_op jit(solution)/shard_map/ppermute | solution.py:259
  45.5 1.9 %update.1 = bf16[32,128,128]{2,1,0:T(8,128)(2,1)} custom-call(bf16[16,160,128]{2,1,0:T(8,128)(2,1)S(1)} %all_to_all.11.got_ref.own_ref, bf16[16,160,128]{2,1,0:T(8,128)(2,1)S(1)} %collective-permute-done.other_ref, bf16[4,128,256]{2,1,0:T(8,128)(2,1)S(1)} %get-tuple-element.16.rows_ref, bf16[4,128,256]{2,1,0:T(8,128)(2,1)S(1)} %get-tuple-element.17.cols_ref), custom_call_target="tpu_custom_call" | custom-call | tf_op jit(solution)/shard_map/update/pallas_call | solution.py:273
  (1 shorter events, 0.0 us)
Async XLA Ops:
  2.1 22.2 %copy-start.3 = (bf16[4,128,128]{2,1,0:T(8,128)(2,1)S(1)}, bf16[4,128,128]{2,1,0:T(8,128)(2,1)}, u32[]{:S(2)}) copy-start(bf16[4,128,128]{2,1,0:T(8,128)(2,1)} %params_ref.1) | copy-start | bytes 393220
  24.4 19.4 %copy-start = (f32[1,4,128,128]{3,2,1,0:T(8,128)S(1)}, f32[1,4,128,128]{3,2,1,0:T(8,128)}, u32[]{:S(2)}) copy-start(f32[1,4,128,128]{3,2,1,0:T(8,128)} %param.6) | copy-start | bytes 786436
  24.4 19.4 %copy-start.1 = (bf16[1,4,128,128]{3,2,1,0:T(8,128)(2,1)S(1)}, bf16[1,4,128,128]{3,2,1,0:T(8,128)(2,1)}, u32[]{:S(2)}) copy-start(bf16[1,4,128,128]{3,2,1,0:T(8,128)(2,1)} %param.5) | copy-start | bytes 393220
  24.4 19.4 %copy-start.2 = (bf16[256,128]{1,0:T(8,128)(2,1)S(1)}, bf16[256,128]{1,0:T(8,128)(2,1)}, u32[]{:S(2)}) copy-start(bf16[256,128]{1,0:T(8,128)(2,1)} %constant.2.clone.down_hbm.down_ref) | copy-start | bytes 196612
  39.0 6.5 %collective-permute-start = (bf16[16,160,128]{2,1,0:T(8,128)(2,1)S(1)}, bf16[16,160,128]{2,1,0:T(8,128)(2,1)S(1)}, u32[]{:S(2)}, u32[]{:S(2)}) collective-permute-start(bf16[16,160,128]{2,1,0:T(8,128)(2,1)S(1)} %all_to_all.11.got_ref.own_ref), channel_id=1, source_target_pairs={{0,8},{8,0},{1,9},{9,1},{2,10},{10,2},{3,11},{11,3},{4,12},{12,4},... | collective-permute-start | bytes 1966088 | tf_op jit(solution)/shard_map/ppermute | solution.py:259

commit v6 on v5

--- a/solution.py
+++ b/solution.py
@@ -15,7 +15,7 @@
 PLANE = ("yh", "yl", "x")
 F32 = jnp.float32
 BF16 = jnp.bfloat16
-Z_ORDER = [(z + 9) % 16 for z in range(16)]
+Z_ORDER = [8, 0, 1, 15, 2, 14, 3, 13, 4, 12, 5, 11, 6, 10, 7, 9]
 PLANE_ORDER = [10] + [i for i in range(15, -1, -1) if i != 10]
 ROWS = 160
 
@@ -93,7 +93,7 @@
 
 
 def bands_kernel(
-    offs_hbm, g_hbm, m_hbm, down_hbm, packed_ref, bands_ref, freq_ref, rows_ref, cols_ref, offs_ref, g_ref, m_ref, down_ref, sems
+    offs_hbm, g_hbm, m_hbm, down_hbm, packed_ref, bands_ref, freq_ref, offs_ref, g_ref, m_ref, down_ref, sems
 ):
     copies = [
         pltpu.make_async_copy(src, dst, sems.at[i])
@@ -113,10 +113,8 @@
     down = down_ref[...]
     cols_high, cols_low = tables(col_freq, down)
     cols = jnp.concatenate([cols_high, cols_low], axis=1)
-    cols_ref[...] = stacked(cols_high, cols_low)
     cols = jnp.concatenate([cols, cols], axis=0)
     rows = dot_nt(picks.astype(BF16), down).astype(BF16)
-    rows_ref[...] = jnp.concatenate(tables(row_freq, down), axis=1)
     row = iota((BAND, TILE), 0)
     freq_ref[...] = jnp.where(row == 0, row_freq, col_freq).astype(F32).astype(BF16)
     copies[2].wait()
@@ -154,17 +152,18 @@
     return PLANE_ORDER.index(8 * yh + 4 * (s % 2) + s // 2)
 
 
-def momentum_kernel(g_ref, m_ref, bands_ref, rows_ref, cols_ref, got_ref, down_ref, out_ref, all_rows_ref, all_cols_ref):
+def momentum_kernel(g_ref, m_ref, bands_ref, freq_ref, got_ref, down_ref, out_ref, all_rows_ref, all_cols_ref):
     lane = iota((1, TILE), 1)
     bands = bands_ref[...]
     diagonal = [jnp.where(lane // BAND == t, bands, 0.0) for t in range(4)]
     diagonal = jnp.concatenate(diagonal + [jnp.zeros((64, TILE), F32)], axis=0)
-    half = wide(fold(dot(rows_ref[...], weights(diagonal))))
-    cols = cols_ref[...]
+    down = down_ref[...]
+    own = freq_ref[...].astype(F32).astype(jnp.int32)
+    half = wide(fold(dot(jnp.concatenate(tables(own[0:1], down), axis=1), weights(diagonal))))
+    cols = stacked(*tables(own[1:2], down))
     for t, mask in enumerate(masks(4, BF16)):
         moment = 0.9 * m_ref[t] + g_ref[t].astype(F32)
         out_ref[t] = moment - fold(dot_nt(half * mask, cols))
-    down = down_ref[...]
     for g in range(4):
         freqs = [got_ref[source(0, s), 144:160].astype(F32).astype(jnp.int32) for s in (2 * g, 2 * g + 1)]
         freqs = jnp.where(lane < 64, freqs[0], freqs[1])
@@ -225,17 +224,15 @@
 def per_device(gradients, momentum, params, band_offsets):
     down = jnp.asarray(split_table())
     g, m = gradients[0], momentum[0]
-    packed, bands, freq, rows, cols = pl.pallas_call(
+    packed, bands, freq = pl.pallas_call(
         bands_kernel,
         out_shape=(
             shape((8, TILE), F32),
             shape((BAND, TILE), F32),
             shape((BAND, TILE), BF16),
-            shape((TILE, 2 * TILE), BF16),
-            shape((2 * TILE, 2 * TILE), BF16),
         ),
         in_specs=[HBM] * 4,
-        out_specs=(VMEM,) * 5,
+        out_specs=(VMEM,) * 3,
         scratch_shapes=[
             pltpu.SMEM((2, 4), jnp.int32),
             pltpu.VMEM((4, TILE, TILE), BF16),
@@ -264,12 +261,12 @@
             shape((4, TILE, 2 * TILE), BF16),
             shape((4, TILE, 2 * TILE), BF16),
         ),
-        in_specs=[VMEM] * 7,
+        in_specs=[VMEM] * 6,
         out_specs=(VMEM,) * 3,
         compiler_params=PARAMS,
         cost_estimate=pl.CostEstimate(flops=200_000_000, bytes_accessed=700_000, transcendentals=0),
         name="momentum",
-    )(g, m, bands, rows, cols, own, down)
+    )(g, m, bands, freq, own, down)
     whole = pl.pallas_call(
         update_kernel,
         out_shape=shape((32, TILE, TILE), BF16),

time: 47.6 us -> 47.3 us (level)
  transfers between devices with their start and end apart: 1 -> 1, of which waited for: 1 -> 1; matrix products, arithmetic and copies ran while one was open for 0% -> 0% of each run, Pallas kernels for 2% -> 3%
where the time goes in v6:
time: 47.3 us; the launch traced here: 47.1 us
  blocking collectives  36.7 us (78%)
  Pallas kernels  4.67 us (10%)
  starting transfers between devices  4.63 us (10%)
  between operations  0.71 us (2%)
    all_to_all x1, blocking collectives, per_device(): lax.all_to_all(jnp.broadcast_to(packed[None], (16, 8, TILE)), 'z', 0, 0,...  22 us
    all_to_all x1, blocking collectives, per_device(): own = lax.all_to_all(blocks, PLANE, 0, 0, axis_index_groups=[PLANE_ORDER])  14.7 us
    ppermute x1, starting transfers between devices, per_device(): other = lax.ppermute(own, 'core', [(0, 1), (1, 0)])  4.63 us
    pallas_call x1, Pallas kernels, per_device(): pl.pallas_call(update_kernel, out_shape=shape((32, TILE, TILE), BF16), in...  1.88 us
    pallas_call x1, Pallas kernels, per_device(): pl.pallas_call(bands_kernel, out_shape=(shape((8, TILE), F32), shape((BAN...  1.45 us
    pallas_call x1, Pallas kernels, per_device(): pl.pallas_call(momentum_kernel, out_shape=(shape((4, TILE, TILE), F32), s...  1.25 us
  transfers between devices with their start and end apart: 1, of which 1 were waited for; matrix products, arithmetic and copies ran while one was open for 0% of the time, Pallas kernels for 3%

profile of v6, /device:TPU:1, one launch (start us, length us, event | category | flops | bytes accessed | tf_op | source)
XLA Modules:
  0.0 47.1 jit_solution(2470308430055523064)
XLA Ops:
  0.6 1.4 %bands.1 = (f32[8,128]{1,0:T(8,128)S(1)}, f32[16,128]{1,0:T(8,128)S(1)}, bf16[16,128]{1,0:T(8,128)(2,1)S(1)}) custom-call(s32[2,4]{1,0:T(2,128)} %bitcast.8, bf16[4,128,128]{2,1,0:T(8,128)(2,1)} %bitcast.6, f32[4,128,128]{2,1,0:T(8,128)} %bitcast.4, bf16[256,128]{1,0:T(8,128)(2,1)} %constant.2.clone.down_hbm.down_ref), custom_call_target="tpu_custom_call" | custom-call | tf_op jit(solution)/shard_map/bands/pallas_call | solution.py:227
  2.1 0.0 copy-start.3
  2.1 22.0 %all_to_all.10.got_ref = f32[16,8,128]{2,1,0:T(8,128)S(1)} all-to-all(f32[16,8,128]{2,1,0:T(8,128)S(1)} %broadcast_in_dim.4), channel_id=1, replica_groups={{128,0,16,240,32,224,48,208,64,192,80,176,96,160,112,144},{129,1,17,241..., dimensions={0} | all-to-all | bytes 131072 | tf_op jit(solution)/shard_map/all_to_all | solution.py:246
  24.1 0.0 copy-done.3
  24.1 0.1 blocks.1
  24.2 0.0 copy-start
  24.2 0.0 copy-start.1
  24.2 0.0 copy-start.2
  24.2 14.7 %all_to_all.11.got_ref.own_ref = bf16[16,160,128]{2,1,0:T(8,128)(2,1)S(1)} all-to-all(bf16[16,160,128]{2,1,0:T(8,128)(2,1)S(1)} %blocks.1), channel_id=1, replica_groups={{260,263,261,259,257,262,258,256,7,5,3,1,6,4,2,0},{268,271,269,267,265,..., dimensions={0} | all-to-all | bytes 1310720 | tf_op jit(solution)/shard_map/all_to_all | solution.py:255
  38.9 4.6 %collective-permute-start = (bf16[16,160,128]{2,1,0:T(8,128)(2,1)S(1)}, bf16[16,160,128]{2,1,0:T(8,128)(2,1)S(1)}, u32[]{:S(2)}, u32[]{:S(2)}) collective-permute-start(bf16[16,160,128]{2,1,0:T(8,128)(2,1)S(1)} %all_to_all.11.got_ref.own_ref), channel_id=1, source_target_pairs={{0,8},{8,0},{1,9},{9,1},{2,10},{10,2},{3,11},{11,3},{4,12},{12,4},... | collective-permute-start | bytes 1966088 | tf_op jit(solution)/shard_map/ppermute | solution.py:256
  43.5 0.0 copy-done
  43.5 0.0 copy-done.1
  43.6 0.0 copy-done.2
  43.6 1.2 %momentum.1 = (f32[4,128,128]{2,1,0:T(8,128)}, bf16[4,128,256]{2,1,0:T(8,128)(2,1)S(1)}, bf16[4,128,256]{2,1,0:T(8,128)(2,1)S(1)}) custom-call(bf16[4,128,128]{2,1,0:T(8,128)(2,1)S(1)} %bitcast.7, f32[4,128,128]{2,1,0:T(8,128)S(1)} %bitcast.5, f32[16,128]{1,0:T(8,128)S(1)} %get-tuple-element.8.bands_ref, bf16[16,128]{1,0:T(8,128)(2,1)S(1)} %get-tuple-element.9.freq_ref, ...), custom_call_target="tpu_custom_call" | custom-call | flops 200000000 | bytes 700000 | tf_op jit(solution)/shard_map/momentum/pallas_call | solution.py:257
  44.8 0.4 collective-permute-done.other_ref
  45.2 1.9 %update.1 = bf16[32,128,128]{2,1,0:T(8,128)(2,1)} custom-call(bf16[16,160,128]{2,1,0:T(8,128)(2,1)S(1)} %all_to_all.11.got_ref.own_ref, bf16[16,160,128]{2,1,0:T(8,128)(2,1)S(1)} %collective-permute-done.other_ref, bf16[4,128,256]{2,1,0:T(8,128)(2,1)S(1)} %get-tuple-element.12.rows_ref, bf16[4,128,256]{2,1,0:T(8,128)(2,1)S(1)} %get-tuple-element.13.cols_ref), custom_call_target="tpu_custom_call" | custom-call | tf_op jit(solution)/shard_map/update/pallas_call | solution.py:270
  (1 shorter events, 0.0 us)
Async XLA Ops:
  2.1 22.0 %copy-start.3 = (bf16[4,128,128]{2,1,0:T(8,128)(2,1)S(1)}, bf16[4,128,128]{2,1,0:T(8,128)(2,1)}, u32[]{:S(2)}) copy-start(bf16[4,128,128]{2,1,0:T(8,128)(2,1)} %params_ref.1) | copy-start | bytes 393220
  24.2 19.4 %copy-start = (f32[1,4,128,128]{3,2,1,0:T(8,128)S(1)}, f32[1,4,128,128]{3,2,1,0:T(8,128)}, u32[]{:S(2)}) copy-start(f32[1,4,128,128]{3,2,1,0:T(8,128)} %param.6) | copy-start | bytes 786436
  24.2 19.4 %copy-start.1 = (bf16[1,4,128,128]{3,2,1,0:T(8,128)(2,1)S(1)}, bf16[1,4,128,128]{3,2,1,0:T(8,128)(2,1)}, u32[]{:S(2)}) copy-start(bf16[1,4,128,128]{3,2,1,0:T(8,128)(2,1)} %param.5) | copy-start | bytes 393220
  24.2 19.4 %copy-start.2 = (bf16[256,128]{1,0:T(8,128)(2,1)S(1)}, bf16[256,128]{1,0:T(8,128)(2,1)}, u32[]{:S(2)}) copy-start(bf16[256,128]{1,0:T(8,128)(2,1)} %constant.2.clone.down_hbm.down_ref) | copy-start | bytes 196612
  38.9 6.3 %collective-permute-start = (bf16[16,160,128]{2,1,0:T(8,128)(2,1)S(1)}, bf16[16,160,128]{2,1,0:T(8,128)(2,1)S(1)}, u32[]{:S(2)}, u32[]{:S(2)}) collective-permute-start(bf16[16,160,128]{2,1,0:T(8,128)(2,1)S(1)} %all_to_all.11.got_ref.own_ref), channel_id=1, source_target_pairs={{0,8},{8,0},{1,9},{9,1},{2,10},{10,2},{3,11},{11,3},{4,12},{12,4},... | collective-permute-start | bytes 1966088 | tf_op jit(solution)/shard_map/ppermute | solution.py:256

commit v7 on v6

--- a/solution.py
+++ b/solution.py
@@ -169,7 +169,14 @@
         freqs = jnp.where(lane < 64, freqs[0], freqs[1])
         all_rows_ref[g] = jnp.concatenate(tables(freqs[0:1], down), axis=1)
         picks = (iota((TILE, TILE), 0) == freqs[1:2]).astype(F32).T.astype(BF16)
-        all_cols_ref[g] = dot_nt(picks, down).astype(BF16)
+        both = dot_nt(picks, down)
+        odd = (iota((TILE, TILE), 0) // BAND) % 2 == 1
+        for sh in range(2):
+            parts = []
+            for part in (both[:, :TILE], both[:, TILE:]):
+                spread = jnp.concatenate([jnp.where(odd, 0.0, part), jnp.where(odd, part, 0.0)], axis=1)
+                parts += [spread[64 * sh : 64 * sh + 64]] * 2
+            all_cols_ref[2 * g + sh] = jnp.concatenate(parts, axis=0).astype(BF16)
 
 
 def update_kernel(own_ref, other_ref, rows_ref, cols_ref, out_hbm, out_ref, sems):
@@ -192,24 +199,28 @@
     high, low = pieces(squares)
     mean = (dot(high, same) + dot(low, same)) * (1.0 / (TILE * TILE))
     inverse = 1.0 / jnp.sqrt(mean + 1e-06)
-    lanes = (iota((1, 2 * TILE), 1) % TILE) // BAND
-    order = [(ref, half_of, sh, yh) for sh in range(2) for ref, half_of in ((own_ref, core), (other_ref, 1 - core)) for yh in range(2)]
+    pair = (iota((1, 2 * TILE), 1) % 64) // (2 * BAND)
+    order = ((own_ref, core), (other_ref, 1 - core))
     copies = []
     for g in range(4):
-        half = wide(halves[g] * inverse[g : g + 1])
-        left = jnp.concatenate(
-            [half * (lanes == 4 * sh + 2 * half_of + yh).astype(F32).astype(BF16) for _, half_of, sh, yh in order], axis=0
-        )
-        cols = cols_ref[g]
-        update = fold(dot(left, jnp.concatenate([cols, cols], axis=0)))
-        for i, (ref, half_of, sh, yh) in enumerate(order):
+        high, low = [p.astype(F32) for p in pieces(halves[g] * inverse[g : g + 1])]
+        for sh in range(2):
             s = 2 * g + sh
-            params = ref[source(yh, s), :128].astype(F32)
-            out_ref[4 * s + 2 * half_of + yh] = (params - update[TILE * i : TILE * i + TILE]).astype(BF16)
-            if i % 4 == 3:
-                tiles = pl.ds(4 * s, 4)
-                copies.append(pltpu.make_async_copy(out_ref.at[tiles], out_hbm.at[tiles], sems.at[s]))
-                copies[-1].start()
+            if sh == 0:
+                half = jnp.where(first, high, pltpu.roll(low, 64, 1)).astype(BF16)
+            else:
+                half = jnp.where(first, pltpu.roll(high, 64, 1), low).astype(BF16)
+            half = jnp.concatenate([half, half], axis=1)
+            left = jnp.concatenate([half * (pair == half_of).astype(F32).astype(BF16) for _, half_of in order], axis=0)
+            update = dot(left, cols_ref[s])
+            for i, (ref, half_of) in enumerate(order):
+                for yh in range(2):
+                    params = ref[source(yh, s), :128].astype(F32)
+                    own = update[TILE * i : TILE * i + TILE, TILE * yh : TILE * yh + TILE]
+                    out_ref[4 * s + 2 * half_of + yh] = (params - own).astype(BF16)
+            tiles = pl.ds(4 * s, 4)
+            copies.append(pltpu.make_async_copy(out_ref.at[tiles], out_hbm.at[tiles], sems.at[s]))
+            copies[-1].start()
     for copy in copies:
         copy.wait()
 
@@ -259,7 +270,7 @@
         out_shape=(
             shape((4, TILE, TILE), F32),
             shape((4, TILE, 2 * TILE), BF16),
-            shape((4, TILE, 2 * TILE), BF16),
+            shape((8, 2 * TILE, 2 * TILE), BF16),
         ),
         in_specs=[VMEM] * 6,
         out_specs=(VMEM,) * 3,

time: 47.3 us -> 47.1 us (level)
  no operation moved by 1% of the time
where the time goes in v7:
time: 47.1 us; the launch traced here: 46.9 us
  blocking collectives  36.7 us (78%)
  starting transfers between devices  4.63 us (10%)
  Pallas kernels  4.46 us (9%)
  between operations  0.71 us (2%)
    all_to_all x1, blocking collectives, per_device(): lax.all_to_all(jnp.broadcast_to(packed[None], (16, 8, TILE)), 'z', 0, 0,...  22 us
    all_to_all x1, blocking collectives, per_device(): own = lax.all_to_all(blocks, PLANE, 0, 0, axis_index_groups=[PLANE_ORDER])  14.7 us
    ppermute x1, starting transfers between devices, per_device(): other = lax.ppermute(own, 'core', [(0, 1), (1, 0)])  4.63 us
    pallas_call x1, Pallas kernels, per_device(): pl.pallas_call(update_kernel, out_shape=shape((32, TILE, TILE), BF16), in...  1.65 us
    pallas_call x1, Pallas kernels, per_device(): pl.pallas_call(bands_kernel, out_shape=(shape((8, TILE), F32), shape((BAN...  1.45 us
    pallas_call x1, Pallas kernels, per_device(): pl.pallas_call(momentum_kernel, out_shape=(shape((4, TILE, TILE), F32), s...  1.27 us
  transfers between devices with their start and end apart: 1, of which 1 were waited for; matrix products, arithmetic and copies ran while one was open for 0% of the time, Pallas kernels for 3%

profile of v7, /device:TPU:1, one launch (start us, length us, event | category | flops | bytes accessed | tf_op | source)
XLA Modules:
  0.0 46.9 jit_solution(16174746627901163523)
XLA Ops:
  0.6 1.4 %bands.1 = (f32[8,128]{1,0:T(8,128)S(1)}, f32[16,128]{1,0:T(8,128)S(1)}, bf16[16,128]{1,0:T(8,128)(2,1)S(1)}) custom-call(s32[2,4]{1,0:T(2,128)} %bitcast.8, bf16[4,128,128]{2,1,0:T(8,128)(2,1)} %bitcast.6, f32[4,128,128]{2,1,0:T(8,128)} %bitcast.4, bf16[256,128]{1,0:T(8,128)(2,1)} %constant.2.clone.down_hbm.down_ref), custom_call_target="tpu_custom_call" | custom-call | tf_op jit(solution)/shard_map/bands/pallas_call | solution.py:238
  2.1 0.0 copy-start.3
  2.1 22.0 %all_to_all.10.got_ref = f32[16,8,128]{2,1,0:T(8,128)S(1)} all-to-all(f32[16,8,128]{2,1,0:T(8,128)S(1)} %broadcast_in_dim.4), channel_id=1, replica_groups={{128,0,16,240,32,224,48,208,64,192,80,176,96,160,112,144},{129,1,17,241..., dimensions={0} | all-to-all | bytes 131072 | tf_op jit(solution)/shard_map/all_to_all | solution.py:257
  24.1 0.0 copy-done.3
  24.1 0.1 blocks.1
  24.2 0.0 copy-start
  24.2 0.0 copy-start.1
  24.2 0.0 copy-start.2
  24.2 14.7 %all_to_all.11.got_ref.own_ref = bf16[16,160,128]{2,1,0:T(8,128)(2,1)S(1)} all-to-all(bf16[16,160,128]{2,1,0:T(8,128)(2,1)S(1)} %blocks.1), channel_id=1, replica_groups={{260,263,261,259,257,262,258,256,7,5,3,1,6,4,2,0},{268,271,269,267,265,..., dimensions={0} | all-to-all | bytes 1310720 | tf_op jit(solution)/shard_map/all_to_all | solution.py:266
  38.9 4.6 %collective-permute-start = (bf16[16,160,128]{2,1,0:T(8,128)(2,1)S(1)}, bf16[16,160,128]{2,1,0:T(8,128)(2,1)S(1)}, u32[]{:S(2)}, u32[]{:S(2)}) collective-permute-start(bf16[16,160,128]{2,1,0:T(8,128)(2,1)S(1)} %all_to_all.11.got_ref.own_ref), channel_id=1, source_target_pairs={{0,8},{8,0},{1,9},{9,1},{2,10},{10,2},{3,11},{11,3},{4,12},{12,4},... | collective-permute-start | bytes 1966088 | tf_op jit(solution)/shard_map/ppermute | solution.py:267
  43.5 0.0 copy-done
  43.5 0.0 copy-done.1
  43.6 0.0 copy-done.2
  43.6 1.3 %momentum.1 = (f32[4,128,128]{2,1,0:T(8,128)}, bf16[4,128,256]{2,1,0:T(8,128)(2,1)S(1)}, bf16[8,256,256]{2,1,0:T(8,128)(2,1)S(1)}) custom-call(bf16[4,128,128]{2,1,0:T(8,128)(2,1)S(1)} %bitcast.7, f32[4,128,128]{2,1,0:T(8,128)S(1)} %bitcast.5, f32[16,128]{1,0:T(8,128)S(1)} %get-tuple-element.8.bands_ref, bf16[16,128]{1,0:T(8,128)(2,1)S(1)} %get-tuple-element.9.freq_ref, ...), custom_call_target="tpu_custom_call" | custom-call | flops 200000000 | bytes 700000 | tf_op jit(solution)/shard_map/momentum/pallas_call | solution.py:268
  44.8 0.4 collective-permute-done.other_ref
  45.2 1.6 %update.1 = bf16[32,128,128]{2,1,0:T(8,128)(2,1)} custom-call(bf16[16,160,128]{2,1,0:T(8,128)(2,1)S(1)} %all_to_all.11.got_ref.own_ref, bf16[16,160,128]{2,1,0:T(8,128)(2,1)S(1)} %collective-permute-done.other_ref, bf16[4,128,256]{2,1,0:T(8,128)(2,1)S(1)} %get-tuple-element.12.rows_ref, bf16[8,256,256]{2,1,0:T(8,128)(2,1)S(1)} %get-tuple-element.13.cols_ref), custom_call_target="tpu_custom_call" | custom-call | tf_op jit(solution)/shard_map/update/pallas_call | solution.py:281
  (1 shorter events, 0.0 us)
Async XLA Ops:
  2.1 22.0 %copy-start.3 = (bf16[4,128,128]{2,1,0:T(8,128)(2,1)S(1)}, bf16[4,128,128]{2,1,0:T(8,128)(2,1)}, u32[]{:S(2)}) copy-start(bf16[4,128,128]{2,1,0:T(8,128)(2,1)} %params_ref.1) | copy-start | bytes 393220
  24.2 19.4 %copy-start = (f32[1,4,128,128]{3,2,1,0:T(8,128)S(1)}, f32[1,4,128,128]{3,2,1,0:T(8,128)}, u32[]{:S(2)}) copy-start(f32[1,4,128,128]{3,2,1,0:T(8,128)} %param.6) | copy-start | bytes 786436
  24.2 19.4 %copy-start.1 = (bf16[1,4,128,128]{3,2,1,0:T(8,128)(2,1)S(1)}, bf16[1,4,128,128]{3,2,1,0:T(8,128)(2,1)}, u32[]{:S(2)}) copy-start(bf16[1,4,128,128]{3,2,1,0:T(8,128)(2,1)} %param.5) | copy-start | bytes 393220
  24.2 19.4 %copy-start.2 = (bf16[256,128]{1,0:T(8,128)(2,1)S(1)}, bf16[256,128]{1,0:T(8,128)(2,1)}, u32[]{:S(2)}) copy-start(bf16[256,128]{1,0:T(8,128)(2,1)} %constant.2.clone.down_hbm.down_ref) | copy-start | bytes 196612
  38.9 6.3 %collective-permute-start = (bf16[16,160,128]{2,1,0:T(8,128)(2,1)S(1)}, bf16[16,160,128]{2,1,0:T(8,128)(2,1)S(1)}, u32[]{:S(2)}, u32[]{:S(2)}) collective-permute-start(bf16[16,160,128]{2,1,0:T(8,128)(2,1)S(1)} %all_to_all.11.got_ref.own_ref), channel_id=1, source_target_pairs={{0,8},{8,0},{1,9},{9,1},{2,10},{10,2},{3,11},{11,3},{4,12},{12,4},... | collective-permute-start | bytes 1966088 | tf_op jit(solution)/shard_map/ppermute | solution.py:267

commit v8 on v7

--- a/solution.py
+++ b/solution.py
@@ -120,9 +120,10 @@
     copies[2].wait()
     copies[3].wait()
     right = jnp.zeros((TILE, TILE), F32)
+    moments = jnp.concatenate([wide(0.9 * m_ref[t] + g_ref[t].astype(F32)) for t in range(4)], axis=0)
+    products = fold(dot(moments, cols))
     for t in range(4):
-        moment = 0.9 * m_ref[t] + g_ref[t].astype(F32)
-        right = jnp.where(slot == t, fold(dot(wide(moment), cols)), right)
+        right = jnp.where(slot == t, products[TILE * t : TILE * t + TILE], right)
     every = fold(dot(rows, weights(right)))
     bands = jnp.zeros((BAND, TILE), F32)
     for t in range(4):

time: 47.1 us -> 47.1 us (level)
  no operation moved by 1% of the time
where the time goes in v8:
time: 47.1 us; the launch traced here: 46.9 us
  blocking collectives  36.6 us (78%)
  starting transfers between devices  4.63 us (10%)
  Pallas kernels  4.48 us (10%)
  between operations  0.71 us (2%)
    all_to_all x1, blocking collectives, per_device(): lax.all_to_all(jnp.broadcast_to(packed[None], (16, 8, TILE)), 'z', 0, 0,...  22 us
    all_to_all x1, blocking collectives, per_device(): own = lax.all_to_all(blocks, PLANE, 0, 0, axis_index_groups=[PLANE_ORDER])  14.7 us
    ppermute x1, starting transfers between devices, per_device(): other = lax.ppermute(own, 'core', [(0, 1), (1, 0)])  4.63 us
    pallas_call x1, Pallas kernels, per_device(): pl.pallas_call(update_kernel, out_shape=shape((32, TILE, TILE), BF16), in...  1.65 us
    pallas_call x1, Pallas kernels, per_device(): pl.pallas_call(bands_kernel, out_shape=(shape((8, TILE), F32), shape((BAN...  1.47 us
    pallas_call x1, Pallas kernels, per_device(): pl.pallas_call(momentum_kernel, out_shape=(shape((4, TILE, TILE), F32), s...  1.27 us
  transfers between devices with their start and end apart: 1, of which 1 were waited for; matrix products, arithmetic and copies ran while one was open for 0% of the time, Pallas kernels for 3%

profile of v8, /device:TPU:1, one launch (start us, length us, event | category | flops | bytes accessed | tf_op | source)
XLA Modules:
  0.0 46.9 jit_solution(3691550201325478356)
XLA Ops:
  0.6 1.5 %bands.1 = (f32[8,128]{1,0:T(8,128)S(1)}, f32[16,128]{1,0:T(8,128)S(1)}, bf16[16,128]{1,0:T(8,128)(2,1)S(1)}) custom-call(s32[2,4]{1,0:T(2,128)} %bitcast.8, bf16[4,128,128]{2,1,0:T(8,128)(2,1)} %bitcast.6, f32[4,128,128]{2,1,0:T(8,128)} %bitcast.4, bf16[256,128]{1,0:T(8,128)(2,1)} %constant.2.clone.down_hbm.down_ref), custom_call_target="tpu_custom_call" | custom-call | tf_op jit(solution)/shard_map/bands/pallas_call | solution.py:239
  2.1 0.0 copy-start.3
  2.1 22.0 %all_to_all.10.got_ref = f32[16,8,128]{2,1,0:T(8,128)S(1)} all-to-all(f32[16,8,128]{2,1,0:T(8,128)S(1)} %broadcast_in_dim.4), channel_id=1, replica_groups={{128,0,16,240,32,224,48,208,64,192,80,176,96,160,112,144},{129,1,17,241..., dimensions={0} | all-to-all | bytes 131072 | tf_op jit(solution)/shard_map/all_to_all | solution.py:258
  24.1 0.0 copy-done.3
  24.1 0.1 blocks.1
  24.2 0.0 copy-start
  24.2 0.0 copy-start.1
  24.2 0.0 copy-start.2
  24.2 14.7 %all_to_all.11.got_ref.own_ref = bf16[16,160,128]{2,1,0:T(8,128)(2,1)S(1)} all-to-all(bf16[16,160,128]{2,1,0:T(8,128)(2,1)S(1)} %blocks.1), channel_id=1, replica_groups={{260,263,261,259,257,262,258,256,7,5,3,1,6,4,2,0},{268,271,269,267,265,..., dimensions={0} | all-to-all | bytes 1310720 | tf_op jit(solution)/shard_map/all_to_all | solution.py:267
  38.9 4.6 %collective-permute-start = (bf16[16,160,128]{2,1,0:T(8,128)(2,1)S(1)}, bf16[16,160,128]{2,1,0:T(8,128)(2,1)S(1)}, u32[]{:S(2)}, u32[]{:S(2)}) collective-permute-start(bf16[16,160,128]{2,1,0:T(8,128)(2,1)S(1)} %all_to_all.11.got_ref.own_ref), channel_id=1, source_target_pairs={{0,8},{8,0},{1,9},{9,1},{2,10},{10,2},{3,11},{11,3},{4,12},{12,4},... | collective-permute-start | bytes 1966088 | tf_op jit(solution)/shard_map/ppermute | solution.py:268
  43.6 0.0 copy-done
  43.6 0.0 copy-done.1
  43.6 0.0 copy-done.2
  43.6 1.3 %momentum.1 = (f32[4,128,128]{2,1,0:T(8,128)}, bf16[4,128,256]{2,1,0:T(8,128)(2,1)S(1)}, bf16[8,256,256]{2,1,0:T(8,128)(2,1)S(1)}) custom-call(bf16[4,128,128]{2,1,0:T(8,128)(2,1)S(1)} %bitcast.7, f32[4,128,128]{2,1,0:T(8,128)S(1)} %bitcast.5, f32[16,128]{1,0:T(8,128)S(1)} %get-tuple-element.8.bands_ref, bf16[16,128]{1,0:T(8,128)(2,1)S(1)} %get-tuple-element.9.freq_ref, ...), custom_call_target="tpu_custom_call" | custom-call | flops 200000000 | bytes 700000 | tf_op jit(solution)/shard_map/momentum/pallas_call | solution.py:269
  44.9 0.4 collective-permute-done.other_ref
  45.3 1.6 %update.1 = bf16[32,128,128]{2,1,0:T(8,128)(2,1)} custom-call(bf16[16,160,128]{2,1,0:T(8,128)(2,1)S(1)} %all_to_all.11.got_ref.own_ref, bf16[16,160,128]{2,1,0:T(8,128)(2,1)S(1)} %collective-permute-done.other_ref, bf16[4,128,256]{2,1,0:T(8,128)(2,1)S(1)} %get-tuple-element.12.rows_ref, bf16[8,256,256]{2,1,0:T(8,128)(2,1)S(1)} %get-tuple-element.13.cols_ref), custom_call_target="tpu_custom_call" | custom-call | tf_op jit(solution)/shard_map/update/pallas_call | solution.py:282
  (1 shorter events, 0.0 us)
Async XLA Ops:
  2.1 22.0 %copy-start.3 = (bf16[4,128,128]{2,1,0:T(8,128)(2,1)S(1)}, bf16[4,128,128]{2,1,0:T(8,128)(2,1)}, u32[]{:S(2)}) copy-start(bf16[4,128,128]{2,1,0:T(8,128)(2,1)} %params_ref.1) | copy-start | bytes 393220
  24.2 19.4 %copy-start = (f32[1,4,128,128]{3,2,1,0:T(8,128)S(1)}, f32[1,4,128,128]{3,2,1,0:T(8,128)}, u32[]{:S(2)}) copy-start(f32[1,4,128,128]{3,2,1,0:T(8,128)} %param.6) | copy-start | bytes 786436
  24.2 19.4 %copy-start.1 = (bf16[1,4,128,128]{3,2,1,0:T(8,128)(2,1)S(1)}, bf16[1,4,128,128]{3,2,1,0:T(8,128)(2,1)}, u32[]{:S(2)}) copy-start(bf16[1,4,128,128]{3,2,1,0:T(8,128)(2,1)} %param.5) | copy-start | bytes 393220
  24.2 19.4 %copy-start.2 = (bf16[256,128]{1,0:T(8,128)(2,1)S(1)}, bf16[256,128]{1,0:T(8,128)(2,1)}, u32[]{:S(2)}) copy-start(bf16[256,128]{1,0:T(8,128)(2,1)} %constant.2.clone.down_hbm.down_ref) | copy-start | bytes 196612
  38.9 6.3 %collective-permute-start = (bf16[16,160,128]{2,1,0:T(8,128)(2,1)S(1)}, bf16[16,160,128]{2,1,0:T(8,128)(2,1)S(1)}, u32[]{:S(2)}, u32[]{:S(2)}) collective-permute-start(bf16[16,160,128]{2,1,0:T(8,128)(2,1)S(1)} %all_to_all.11.got_ref.own_ref), channel_id=1, source_target_pairs={{0,8},{8,0},{1,9},{9,1},{2,10},{10,2},{3,11},{11,3},{4,12},{12,4},... | collective-permute-start | bytes 1966088 | tf_op jit(solution)/shard_map/ppermute | solution.py:268
